TPU v7x, 768 devices: a whole 4x8x12 slice. The times are simulated.
768 devices in a mesh: crop: 96 (over z, y_lo, core), branch: 2 (over y_hi), dap: 4 (over x).
Axes of the slice: x: 4, y: 8 (y_hi: 2, y_lo: 4; y = y_hi * 4 + y_lo), z: 12, core: 2. Of those that a mesh axis runs over, the one named last changes fastest.
Arguments:
- homolog_matrix: bfloat16 [6144, 128, 256], P(('crop', 'dap')), parts along dimension 0, may hold values from -6 to 6
- homolog_entry_flags: int32 [6144, 128], P(('crop', 'dap')), parts along dimension 0, may hold values 0 or 1
- couple_matrix: bfloat16 [12288, 128, 128], P(('crop', 'dap')), parts along dimension 0, may hold values from -6 to 6
- window_amino_flags: int32 [12288], P('crop'), parts along dimension 0, may hold values from 0 to 1, as said below
- pairwise_standardize_scaling: float32 [256], replicated, may hold values from 0.1 to 1.9
- pairwise_standardize_offset: float32 [256], replicated, may hold values from -3 to 3
- pairwise_factor_matrices: bfloat16 [256, 64], replicated, may hold values from -0.375 to 0.375
- pairwise_final_matrix: bfloat16 [1024, 128], replicated, may hold values from -0.75 to 0.75
- pairwise_final_offset: float32 [128], replicated, may hold values from -3 to 3
- trimul_entry_standardize_scaling: float32 [128], replicated, may hold values from 0.1 to 1.9
- trimul_entry_standardize_offset: float32 [128], replicated, may hold values from -3 to 3
- trimul_entry_matrices: bfloat16 [128, 640], replicated, may hold values from -0.5 to 0.5
- trimul_entry_offsets: float32 [640], replicated, may hold values from -3 to 3
- trimul_final_standardize_scaling: float32 [128], replicated, may hold values from 0.1 to 1.9
- trimul_final_standardize_offset: float32 [128], replicated, may hold values from -3 to 3
- trimul_final_matrix: bfloat16 [128, 128], replicated, may hold values from -0.5 to 0.5
- trimul_final_offset: float32 [128], replicated, may hold values from -3 to 3
Outputs:
- pair_out: bfloat16 [12288, 128, 128], P(('crop', 'dap'), 'branch'), parts along dimension 0
There are 96 independent parts, one for each index of `crop`. A program takes and returns all parts, laid end to end along the dimension named above; an argument that names none is the same for every part. Nothing has to cross between parts.
Inputs may be any that keep to these rules, and one draw needn't show every extreme that they name: `window_amino_flags`: 1 on the first residues of the crop and 0 on the rest, with at least 64 ones.
All inputs are finite; a program needn't handle non-finite values. No bound on the sum of `homolog_entry_flags` on one device may be relied on, other than what follows from the above.
Results may differ from a plain program's by a relative error of at most 0.0057.
Values may be sent and summed in bfloat16 or wider, within the bound.
No kernel may reach another device: no remote copies, remote signals or barrier semaphores. Data moves between devices by JAX's collectives and lax.ppermute only.
A program may use at most 64 MiB of HBM per device.

v0:
```python
import math

import jax
import jax.numpy as jnp
from jax import lax
from jax.sharding import PartitionSpec as P


def from_everyone(x, axis):
    copies = jnp.broadcast_to(x, (lax.axis_size(axis), *x.shape))
    return lax.all_to_all(copies, axis, split_axis=0, concat_axis=0, tiled=True)


def in_order(pieces, dim):
    pieces = jnp.moveaxis(pieces, 0, dim)
    dims = pieces.shape
    return pieces.reshape(*dims[:dim], dims[dim] * dims[dim + 1], *dims[dim + 2 :])


def gathered_copies(x, axis, dim):
    pieces = from_everyone(x, axis)
    return in_order(pieces, dim)


def in_one_piece(arrays, axis, dim, along):
    columns = [a.reshape(*a.shape[:along], -1) for a in arrays]
    both = jnp.concatenate(columns, axis=along)
    result, at, gathered = (gathered_copies(both, axis, dim), 0, [])
    for a, column in zip(arrays, columns):
        slab = result[..., at : at + column.shape[along]]
        gathered.append(slab.reshape(*slab.shape[:along], *a.shape[along:]))
        at += column.shape[along]
    return tuple(gathered)


def standardize_features(values, gain_vec, bias_vec):
    center = jnp.mean(values, axis=-1, keepdims=True)
    rotated_partner_block = values - center
    spread = jnp.mean(rotated_partner_block * rotated_partner_block, axis=-1, keepdims=True)
    return rotated_partner_block * lax.rsqrt(spread + 1e-05) * gain_vec + bias_vec


def outer_update(left_rows, right_cols, inverse, pairwise_final_matrix, pairwise_final_offset):
    seq_count, own_rows, width_c = left_rows.shape
    columns = right_cols.shape[1]
    block_rows = math.gcd(own_rows, max(1, 512 // columns))
    blocks = own_rows // block_rows
    left_blocks = jnp.transpose(
        left_rows.reshape(seq_count, blocks, block_rows, width_c), (1, 0, 2, 3)
    )
    inverse_blocks = inverse.reshape(blocks, block_rows, columns)

    def one_block(inputs):
        left_block, inverse_block = inputs
        products = jnp.einsum(
            "sic,sjd->ijcd", left_block, right_cols, preferred_element_type=jnp.float32
        )
        averaged = (products * inverse_block[:, :, None, None]).astype(jnp.bfloat16)
        flat = averaged.reshape(block_rows * columns, width_c * width_c)
        update = (
            jnp.dot(flat, pairwise_final_matrix, preferred_element_type=jnp.float32)
            + pairwise_final_offset
        )
        return update.reshape(block_rows, columns, -1).astype(jnp.bfloat16)

    result = lax.map(one_block, (left_blocks, inverse_blocks))
    return result.reshape(own_rows, columns, -1)


def local(
    homolog_matrix,
    homolog_entry_flags,
    couple_matrix,
    window_amino_flags,
    pairwise_standardize_scaling,
    pairwise_standardize_offset,
    pairwise_factor_matrices,
    pairwise_final_matrix,
    pairwise_final_offset,
    trimul_entry_standardize_scaling,
    trimul_entry_standardize_offset,
    trimul_entry_matrices,
    trimul_entry_offsets,
    trimul_final_standardize_scaling,
    trimul_final_standardize_offset,
    trimul_final_matrix,
    trimul_final_offset,
):
    own_rows, residues, pair_width = couple_matrix.shape
    hidden = trimul_final_matrix.shape[0]
    half_cols = residues // 2
    row_start = lax.axis_index("dap") * own_rows
    branch_place = lax.axis_index("branch")
    residue_present = window_amino_flags.astype(jnp.float32)
    row_live = lax.dynamic_slice_in_dim(residue_present, row_start, own_rows, 0)
    own_pair = lax.dynamic_slice_in_dim(couple_matrix, branch_place * half_cols, half_cols, 1)
    col_start = branch_place * half_cols
    always = jnp.asarray(True)
    homolog_subset, homolog_positions, homolog_feature_count = homolog_matrix.shape
    outer_product_width = pairwise_factor_matrices.shape[1] // 2
    sequence_present = homolog_entry_flags.astype(jnp.float32) * residue_present[None, :]

    def project_alignment_rows(discarded_result):
        homolog_standardized = standardize_features(
            homolog_matrix.astype(jnp.float32),
            pairwise_standardize_scaling,
            pairwise_standardize_offset,
        ).astype(jnp.bfloat16)
        mapped = jnp.dot(
            homolog_standardized.reshape(homolog_subset * homolog_positions, homolog_feature_count),
            pairwise_factor_matrices,
            preferred_element_type=jnp.float32,
        )
        mapped = (
            mapped.reshape(homolog_subset, homolog_positions, 2 * outer_product_width)
            * sequence_present[:, :, None]
        )
        return (
            mapped[:, :, :outer_product_width].astype(jnp.bfloat16),
            mapped[:, :, outer_product_width:].astype(jnp.bfloat16),
        )

    def bypass_alignment_update(discarded_result):
        blank = jnp.zeros((homolog_subset, homolog_positions, outer_product_width), jnp.bfloat16)
        return (blank, blank)

    outer_product_left_factor, outer_product_right_factor = lax.cond(
        always, project_alignment_rows, bypass_alignment_update, 0
    )
    live_flags = sequence_present.astype(jnp.bfloat16)
    left_all, right_all, flags_all = in_one_piece(
        (outer_product_left_factor, outer_product_right_factor, live_flags), "dap", 0, 2
    )
    left_rows = lax.dynamic_slice_in_dim(left_all, row_start, own_rows, 1)
    flags_rows = lax.dynamic_slice_in_dim(flags_all, row_start, own_rows, 1)
    flags_cols = lax.dynamic_slice_in_dim(flags_all, col_start, half_cols, 1)
    right_cols = lax.dynamic_slice_in_dim(right_all, col_start, half_cols, 1)

    def compute_outer(discarded_result):
        count = jnp.dot(flags_rows.T, flags_cols, preferred_element_type=jnp.float32)
        inverse = 1.0 / jnp.maximum(count, 1.0)
        return outer_update(
            left_rows, right_cols, inverse, pairwise_final_matrix, pairwise_final_offset
        )

    def skip_outer(discarded_result):
        return jnp.zeros((own_rows, half_cols, pair_width), jnp.bfloat16)

    outer_half = lax.cond(always, compute_outer, skip_outer, 0)
    masked = row_live[:, None, None] * residue_present[None, :, None]

    def project_pair(discarded_result):
        pair_normed = standardize_features(
            couple_matrix.astype(jnp.float32),
            trimul_entry_standardize_scaling,
            trimul_entry_standardize_offset,
        ).astype(jnp.bfloat16)
        mapped = (
            jnp.dot(
                pair_normed.reshape(-1, pair_width),
                trimul_entry_matrices,
                preferred_element_type=jnp.float32,
            )
            + trimul_entry_offsets
        )
        mapped = mapped.reshape(own_rows, residues, -1)
        left_part = (
            jax.nn.sigmoid(mapped[:, :, :hidden]) * mapped[:, :, hidden : 2 * hidden] * masked
        ).astype(jnp.bfloat16)
        right_part = (
            jax.nn.sigmoid(mapped[:, :, 2 * hidden : 3 * hidden])
            * mapped[:, :, 3 * hidden : 4 * hidden]
            * masked
        ).astype(jnp.bfloat16)
        gate_part = jax.nn.sigmoid(
            lax.dynamic_slice_in_dim(mapped[:, :, 4 * hidden :], col_start, half_cols, 1)
        )
        return (left_part, right_part, gate_part)

    def skip_pair(discarded_result):
        blank = jnp.zeros((own_rows, residues, hidden), jnp.bfloat16)
        return (blank, blank, jnp.zeros((own_rows, half_cols, pair_width), jnp.float32))

    left_own, right_own, out_gate = lax.cond(always, project_pair, skip_pair, 0)
    start_sum = jnp.zeros((own_rows, residues, hidden), jnp.float32)

    def add_right(incoming):
        contrib = jnp.einsum("ikc,jkc->ijc", left_own, incoming, preferred_element_type=jnp.float32)
        return contrib

    incoming = lax.all_gather(right_own, "dap", axis=0, tiled=True)
    in_start = jnp.int32(0)
    reached = jnp.logical_and(
        in_start < col_start + half_cols, in_start + incoming.shape[0] > col_start
    )
    reached = jnp.logical_and(reached, always)
    tri_full = lax.cond(
        reached, lambda carried: add_right(incoming), lambda carried: carried, start_sum
    )
    tri_sum = lax.dynamic_slice_in_dim(tri_full, col_start, half_cols, 1)

    def finish(discarded_result):
        tri_mid = standardize_features(
            tri_sum, trimul_final_standardize_scaling, trimul_final_standardize_offset
        ).astype(jnp.bfloat16)
        mixed = jnp.dot(
            tri_mid.reshape(-1, hidden), trimul_final_matrix, preferred_element_type=jnp.float32
        ).reshape(own_rows, half_cols, -1)
        return (out_gate * (mixed + trimul_final_offset)).astype(jnp.bfloat16)

    def skip_finish(discarded_result):
        return jnp.zeros((own_rows, half_cols, pair_width), jnp.bfloat16)

    triangle_half = lax.cond(always, finish, skip_finish, 0)
    total = (
        own_pair.astype(jnp.float32)
        + outer_half.astype(jnp.float32)
        + triangle_half.astype(jnp.float32)
    )
    return total.astype(jnp.bfloat16)


def solution(mesh):
    placed = (
        P(("crop", "dap"), None, None),
        P(("crop", "dap"), None),
        P(("crop", "dap"), None, None),
        P("crop"),
        P(),
        P(),
        P(),
        P(),
        P(),
        P(),
        P(),
        P(),
        P(),
        P(),
        P(),
        P(),
        P(),
    )
    return jax.shard_map(
        local,
        mesh=mesh,
        in_specs=placed,
        out_specs=P(("crop", "dap"), "branch", None),
        check_vma=False,
    )
```

profile of v0, /device:TPU:1, one launch (start us, length us, event | category | flops | bytes accessed | tf_op | source)
XLA Modules:
  0.0 105.0 jit_solution(4777459713550221208)
XLA Ops:
  6.6 0.7 convert_element_type.76
  7.5 1.6 %convert_reduce_fusion = f32[32,128]{1,0:T(8,128)S(1)} fusion(bf16[32,128,128]{2,1,0:T(8,128)(2,1)} %param.23), kind=kLoop, calls=%fused_computation.13 | loop fusion | flops 1044480 | bytes 1064960 | tf_op jit(solution)/shard_map/cond/branch_1_fun/reduce_sum | solution.py:37
  9.1 2.3 %fusion.10 = f32[32,128]{1,0:T(8,128)S(1)} fusion(bf16[32,128,128]{2,1,0:T(8,128)(2,1)} %param.23, f32[32,128]{1,0:T(8,128)S(1)} %broadcast_multiply_fusion.2), kind=kLoop, calls=%fused_computation.20 | loop fusion | flops 2093056 | bytes 1081344 | tf_op jit(solution)/shard_map/cond/branch_1_fun/reduce_sum | solution.py:39
  11.5 1.3 %fusion.13 = bf16[32,128,128]{2,1,0:T(8,128)(2,1)S(1)} fusion(bf16[32,128,128]{2,1,0:T(8,128)(2,1)S(1)} %copy-done.1, f32[128]{0:T(128)S(1)} %copy-done.11, f32[128]{0:T(128)S(1)} %copy-done.12, f32[32,128]{1,0:T(8,128)S(1)} %add_rsqrt_fusion.1, f32[32,128]{1,0:T(8,128)S(1)} %broadcast_multiply_fusion.2), kind=kLoop, calls=%fused_computation.23 | loop fusion | flops 3145728 | bytes 2130944 | tf_op jit(solution)/shard_map/cond/branch_1_fun/convert_element_type | solution.py:157
  12.8 1.5 %convolution_add_fusion.1 = f32[4096,640]{1,0:T(8,128)S(1)} fusion(bf16[4096,128]{1,0:T(8,128)(2,1)S(1)} %bitcast.67, bf16[128,640]{1,0:T(8,128)(2,1)S(1)} %copy-done, f32[640]{0:T(1024)S(1)} %copy-done.6), kind=kOutput, calls=%fused_computation.11 | convolution fusion | flops 673710080 | bytes 11700736 | tf_op jit(solution)/shard_map/cond/branch_1_fun/dot_general | solution.py:159
  14.3 2.7 %fusion.19 = (bf16[32,128,128]{2,1,0:T(8,128)(2,1)}, bf16[32,128,128]{2,1,0:T(8,128)(2,1)}, f32[32,128,128]{2,1,0:T(8,128)}) fusion(f32[32,128,640]{2,1,0:T(8,128)S(1)} %bitcast.65, f32[32,128]{1,0:T(8,128)S(1)} %broadcast_multiply_fusion.1), kind=kLoop, calls=%fused_computation.30 | loop fusion | flops 6291456 | bytes 14696448 | tf_op jit(solution)/shard_map/cond/branch_1_fun/convert_element_type | solution.py:169
  17.1 0.3 convert_reduce_fusion.1
  17.5 0.6 fusion.14
  18.2 1.0 fusion.33
  19.3 1.1 %broadcast_in_dim.8 = bf16[4,16,128,65]{2,1,3,0:T(8,128)(2,1)} broadcast(bf16[16,128,65]{1,0,2:T(8,128)(2,1)S(1)} %copy.39), dimensions={1,2,3} | broadcast | bytes 1331200 | tf_op jit(solution)/shard_map/broadcast_in_dim | solution.py:10
  20.4 4.8 %all-to-all-start = ((bf16[4,16,128,65]{2,1,3,0:T(8,128)(2,1)}), bf16[4,16,128,65]{2,1,3,0:T(8,128)(2,1)S(1)}, u32[]{:S(2)}, u32[]{:S(2)}) async-start(bf16[4,16,128,65]{2,1,3,0:T(8,128)(2,1)} %broadcast_in_dim.8), calls=%async_computation | async-start | bytes 2129920 | tf_op jit(solution)/shard_map/all_to_all | solution.py:11
  25.2 9.8 %all-to-all-done = bf16[4,16,128,65]{2,1,3,0:T(8,128)(2,1)S(1)} async-done(((bf16[4,16,128,65]{2,1,3,0:T(8,128)(2,1)}), bf16[4,16,128,65]{2,1,3,0:T(8,128)(2,1)S(1)}, u32[]{:S(2)}, u32[]{:S(2)}) %all-to-all-start) | async-done | bytes 1064992 | tf_op jit(solution)/shard_map/all_to_all | solution.py:11
  35.1 0.3 copy.40
  35.7 1.1 %copy.41 = bf16[64,32,32]{0,2,1:T(8,128)(2,1)} copy(bf16[64,32,32]{1,0,2:T(8,128)(2,1)S(1)} %constant_dynamic-slice_fusion.1) | data formatting | bytes 262144 | tf_op jit(solution)/shard_map/dynamic_slice | solution.py:134
  36.8 0.2 fusion.35
  37.1 1.0 constant_dynamic-slice_fusion
  38.1 26.1 %while.10 = (s32[]{:T(128)}, bf16[4,8,64,128]{3,2,1,0:T(8,128)(2,1)}, bf16[4,64,8,32]{1,3,2,0:T(8,128)(2,1)}, bf16[64,64,32]{1,0,2:T(8,128)(2,1)}, f32[4,8,64]{2...) while((s32[]{:T(128)}, bf16[4,8,64,128]{3,2,1,0:T(8,128)(2,1)}, ...), condition=%wide.region_3.4_spmd, body=%wide.region_2.3_spmd.sunk | while | flops 202506240 | bytes 7544409 | solution.py:66
  38.1 1.8 %fusion.65 = bf16[8,64,32,32]{1,2,3,0:T(8,128)(2,1)S(1)} fusion(f32[8,64]{1,0:T(8,128)S(1)} %dynamic-slice_bitcast_fusion.2, bf16[64,64,32]{1,0,2:T(8,128)(2,1)} %get-tuple-element.151, bf16[4,64,8,32]{1,3,2,0:T(8,128)(2,1)} %get-tuple-element.150, s32[]{:T(128)} %get-tuple-element.140), kind=kOutput, calls=%fused_computation.1.clone.1 | convolution fusion | flops 68157440 | bytes 1640960 | tf_op jit(solution)/shard_map/cond/branch_1_fun/while/body/eval_jaxpr/sic,sjd->ijcd/dot_general | solution.py:55
  39.8 1.4 %copy.50 = bf16[8,64,32,32]{1,0,3,2:T(8,128)(2,1)S(1)} copy(bf16[8,64,32,32]{1,2,3,0:T(8,128)(2,1)S(1)} %fusion.65) | data formatting | bytes 2097152 | tf_op jit(solution)/shard_map/cond/branch_1_fun/while/body/eval_jaxpr/convert_element_type | solution.py:58
  41.2 1.3 %reshape.140 = bf16[512,1024]{0,1:T(8,128)(2,1)S(1)} reshape(bf16[8,64,32,32]{1,0,3,2:T(8,128)(2,1)S(1)} %copy.50) | data formatting | bytes 2097152 | tf_op jit(solution)/shard_map/cond/branch_1_fun/while/body/eval_jaxpr/reshape | solution.py:59
  42.5 1.5 %fusion.66 = bf16[512,128]{1,0:T(8,128)(2,1)S(1)} fusion(bf16[512,1024]{0,1:T(8,128)(2,1)S(1)} %reshape.140, bf16[1024,128]{1,0:T(8,128)(2,1)} %get-tuple-element.153, f32[128]{0:T(128)S(1)} %get-tuple-element.154), kind=kOutput, calls=%fused_computation.3.clone.1 | convolution fusion | flops 134348800 | bytes 1442304 | tf_op jit(solution)/shard_map/cond/branch_1_fun/while/body/eval_jaxpr/dot_general | solution.py:61
  43.9 0.7 constant_dynamic-update-slice_fusion.2
  44.6 1.8 %fusion.65 = bf16[8,64,32,32]{1,2,3,0:T(8,128)(2,1)S(1)} fusion(f32[8,64]{1,0:T(8,128)S(1)} %dynamic-slice_bitcast_fusion.2, bf16[64,64,32]{1,0,2:T(8,128)(2,1)} %get-tuple-element.151, bf16[4,64,8,32]{1,3,2,0:T(8,128)(2,1)} %get-tuple-element.150, s32[]{:T(128)} %get-tuple-element.140), kind=kOutput, calls=%fused_computation.1.clone.1 | convolution fusion | flops 68157440 | bytes 1640960 | tf_op jit(solution)/shard_map/cond/branch_1_fun/while/body/eval_jaxpr/sic,sjd->ijcd/dot_general | solution.py:55
  46.4 1.4 %copy.50 = bf16[8,64,32,32]{1,0,3,2:T(8,128)(2,1)S(1)} copy(bf16[8,64,32,32]{1,2,3,0:T(8,128)(2,1)S(1)} %fusion.65) | data formatting | bytes 2097152 | tf_op jit(solution)/shard_map/cond/branch_1_fun/while/body/eval_jaxpr/convert_element_type | solution.py:58
  47.8 1.3 %reshape.140 = bf16[512,1024]{0,1:T(8,128)(2,1)S(1)} reshape(bf16[8,64,32,32]{1,0,3,2:T(8,128)(2,1)S(1)} %copy.50) | data formatting | bytes 2097152 | tf_op jit(solution)/shard_map/cond/branch_1_fun/while/body/eval_jaxpr/reshape | solution.py:59
  49.1 1.4 %fusion.66 = bf16[512,128]{1,0:T(8,128)(2,1)S(1)} fusion(bf16[512,1024]{0,1:T(8,128)(2,1)S(1)} %reshape.140, bf16[1024,128]{1,0:T(8,128)(2,1)} %get-tuple-element.153, f32[128]{0:T(128)S(1)} %get-tuple-element.154), kind=kOutput, calls=%fused_computation.3.clone.1 | convolution fusion | flops 134348800 | bytes 1442304 | tf_op jit(solution)/shard_map/cond/branch_1_fun/while/body/eval_jaxpr/dot_general | solution.py:61
  50.5 0.7 constant_dynamic-update-slice_fusion.2
  51.2 1.8 %fusion.65 = bf16[8,64,32,32]{1,2,3,0:T(8,128)(2,1)S(1)} fusion(f32[8,64]{1,0:T(8,128)S(1)} %dynamic-slice_bitcast_fusion.2, bf16[64,64,32]{1,0,2:T(8,128)(2,1)} %get-tuple-element.151, bf16[4,64,8,32]{1,3,2,0:T(8,128)(2,1)} %get-tuple-element.150, s32[]{:T(128)} %get-tuple-element.140), kind=kOutput, calls=%fused_computation.1.clone.1 | convolution fusion | flops 68157440 | bytes 1640960 | tf_op jit(solution)/shard_map/cond/branch_1_fun/while/body/eval_jaxpr/sic,sjd->ijcd/dot_general | solution.py:55
  52.9 1.4 %copy.50 = bf16[8,64,32,32]{1,0,3,2:T(8,128)(2,1)S(1)} copy(bf16[8,64,32,32]{1,2,3,0:T(8,128)(2,1)S(1)} %fusion.65) | data formatting | bytes 2097152 | tf_op jit(solution)/shard_map/cond/branch_1_fun/while/body/eval_jaxpr/convert_element_type | solution.py:58
  54.3 1.3 %reshape.140 = bf16[512,1024]{0,1:T(8,128)(2,1)S(1)} reshape(bf16[8,64,32,32]{1,0,3,2:T(8,128)(2,1)S(1)} %copy.50) | data formatting | bytes 2097152 | tf_op jit(solution)/shard_map/cond/branch_1_fun/while/body/eval_jaxpr/reshape | solution.py:59
  55.6 1.4 %fusion.66 = bf16[512,128]{1,0:T(8,128)(2,1)S(1)} fusion(bf16[512,1024]{0,1:T(8,128)(2,1)S(1)} %reshape.140, bf16[1024,128]{1,0:T(8,128)(2,1)} %get-tuple-element.153, f32[128]{0:T(128)S(1)} %get-tuple-element.154), kind=kOutput, calls=%fused_computation.3.clone.1 | convolution fusion | flops 134348800 | bytes 1442304 | tf_op jit(solution)/shard_map/cond/branch_1_fun/while/body/eval_jaxpr/dot_general | solution.py:61
  57.0 0.7 constant_dynamic-update-slice_fusion.2
  57.7 1.8 %fusion.65 = bf16[8,64,32,32]{1,2,3,0:T(8,128)(2,1)S(1)} fusion(f32[8,64]{1,0:T(8,128)S(1)} %dynamic-slice_bitcast_fusion.2, bf16[64,64,32]{1,0,2:T(8,128)(2,1)} %get-tuple-element.151, bf16[4,64,8,32]{1,3,2,0:T(8,128)(2,1)} %get-tuple-element.150, s32[]{:T(128)} %get-tuple-element.140), kind=kOutput, calls=%fused_computation.1.clone.1 | convolution fusion | flops 68157440 | bytes 1640960 | tf_op jit(solution)/shard_map/cond/branch_1_fun/while/body/eval_jaxpr/sic,sjd->ijcd/dot_general | solution.py:55
  59.4 1.4 %copy.50 = bf16[8,64,32,32]{1,0,3,2:T(8,128)(2,1)S(1)} copy(bf16[8,64,32,32]{1,2,3,0:T(8,128)(2,1)S(1)} %fusion.65) | data formatting | bytes 2097152 | tf_op jit(solution)/shard_map/cond/branch_1_fun/while/body/eval_jaxpr/convert_element_type | solution.py:58
  60.8 1.3 %reshape.140 = bf16[512,1024]{0,1:T(8,128)(2,1)S(1)} reshape(bf16[8,64,32,32]{1,0,3,2:T(8,128)(2,1)S(1)} %copy.50) | data formatting | bytes 2097152 | tf_op jit(solution)/shard_map/cond/branch_1_fun/while/body/eval_jaxpr/reshape | solution.py:59
  62.1 1.4 %fusion.66 = bf16[512,128]{1,0:T(8,128)(2,1)S(1)} fusion(bf16[512,1024]{0,1:T(8,128)(2,1)S(1)} %reshape.140, bf16[1024,128]{1,0:T(8,128)(2,1)} %get-tuple-element.153, f32[128]{0:T(128)S(1)} %get-tuple-element.154), kind=kOutput, calls=%fused_computation.3.clone.1 | convolution fusion | flops 134348800 | bytes 1442304 | tf_op jit(solution)/shard_map/cond/branch_1_fun/while/body/eval_jaxpr/dot_general | solution.py:61
  63.5 0.7 constant_dynamic-update-slice_fusion.2
  64.2 16.9 %all-gather.2.cloned.1.call-done = bf16[128,128,128]{2,1,0:T(8,128)(2,1)} async-done(((bf16[32,128,128]{2,1,0:T(8,128)(2,1)}), bf16[128,128,128]{2,1,0:T(8,128)(2,1)}) %all-gather.2.cloned.1.call-update) | async-done | bytes 4194320 | tf_op jit(solution)/shard_map/all_gather | solution.py:191
  81.1 12.3 %conditional.1 = (f32[32,128,128]{1,0,2:T(8,128)S(1)}) conditional(s32[]{:T(128)} %convert_element_type.82, () %tuple.16, (bf16[128,128,128]{2,1,0:T(8,128)(2,1)}, bf16[32,128,128]{2,1,0:T(8,128)(2,1)}) %tuple.17), branch_computations={%region_6.7_spmd, %region_7.8_spmd} | conditional | flops 134217728 | bytes 22020132 | solution.py:197
  81.1 6.9 %copy.43 = bf16[128,128,128]{1,0,2:T(8,128)(2,1)} copy(bf16[128,128,128]{2,1,0:T(8,128)(2,1)} %get-tuple-element.65) | data formatting | bytes 8388608 | tf_op jit(solution)/shard_map
  88.0 1.0 copy.44
  89.0 4.5 %convolution_bitcast_fusion = f32[32,128,128]{1,0,2:T(8,128)S(1)} fusion(bf16[128,128,128]{1,0,2:T(8,128)(2,1)} %copy.43, bf16[32,128,128]{1,0,2:T(8,128)(2,1)S(1)} %copy.44), kind=kOutput, calls=%fused_computation.10 | convolution fusion | flops 134217728 | bytes 7340032 | tf_op jit(solution)/shard_map/cond/branch_1_fun/ikc,jkc->ijc/dot_general | solution.py:188
  93.4 0.6 dynamic-slice_reduce_fusion
  94.1 0.6 multiply_reduce_fusion
  94.8 0.9 add_convert_fusion
  95.7 0.2 copy-done.2
  96.0 0.7 copy-done.5
  96.7 1.5 %fusion.32 = bf16[32,64,128]{2,1,0:T(8,128)(2,1)} fusion(bf16[32,64,128]{2,1,0:T(8,128)(2,1)S(1)} %bitcast.70, bf16[32,64,128]{1,0,2:T(8,128)(2,1)S(1)} %add_convert_fusion, f32[32,128,128]{2,1,0:T(8,128)S(1)} %copy-done.5, s32[]{:T(128)S(6)} %select_n.4, f32[128]{0:T(128)S(1)} %copy-done.18, bf16[32,128,128]{2,1,0:T(8,128)(2,1)S(1)} %copy-done.2, ...), kind=kOutput, calls=%fused_computation.50 | convolution fusion | flops 70254592 | bytes 3179012 | tf_op jit(solution)/shard_map/cond/branch_1_fun/dot_general | solution.py:206
  (57 shorter events, 0.7 us)
Async XLA Ops:
  6.5 6.2 %copy-start = (bf16[128,640]{1,0:T(8,128)(2,1)S(1)}, bf16[128,640]{1,0:T(8,128)(2,1)}, u32[]{:S(2)}) copy-start(bf16[128,640]{1,0:T(8,128)(2,1)} %param.32) | copy-start | bytes 491524
  6.5 4.9 %copy-start.1 = (bf16[32,128,128]{2,1,0:T(8,128)(2,1)S(1)}, bf16[32,128,128]{2,1,0:T(8,128)(2,1)}, u32[]{:S(2)}) copy-start(bf16[32,128,128]{2,1,0:T(8,128)(2,1)} %param.23) | copy-start | bytes 3145732
  6.5 4.9 %copy-start.12 = (f32[128]{0:T(128)S(1)}, f32[128]{0:T(128)}, u32[]{:S(2)}) copy-start(f32[128]{0:T(128)} %param.30) | copy-start | bytes 1540
  6.5 4.9 %copy-start.11 = (f32[128]{0:T(128)S(1)}, f32[128]{0:T(128)}, u32[]{:S(2)}) copy-start(f32[128]{0:T(128)} %param.31) | copy-start | bytes 1540
  6.5 74.6 %all-gather.2.cloned.1.call-start = ((), (), s32[]{:S(2)}) async-start(), calls=%async_computation.1 | async-start | bytes 5242880 | tf_op jit(solution)/shard_map/all_gather | solution.py:191
  7.5 5.3 %copy-start.6 = (f32[640]{0:T(1024)S(1)}, f32[640]{0:T(1024)}, u32[]{:S(2)}) copy-start(f32[640]{0:T(1024)} %param.33) | copy-start | bytes 7684
  14.3 2.8 %copy-start.4 = (bf16[16,128,256]{2,1,0:T(8,128)(2,1)S(1)}, bf16[16,128,256]{2,1,0:T(8,128)(2,1)}, u32[]{:S(2)}) copy-start(bf16[16,128,256]{2,1,0:T(8,128)(2,1)} %param.21) | copy-start | bytes 3145732
  17.0 1.1 %copy-start.8 = (s32[16,128]{1,0:T(8,128)S(1)}, s32[16,128]{1,0:T(8,128)}, u32[]{:S(2)}) copy-start(s32[16,128]{1,0:T(8,128)} %param.22) | copy-start | bytes 24580
  17.0 1.1 %copy-start.14 = (bf16[256,64]{0,1:T(8,128)(2,1)S(1)}, bf16[256,64]{0,1:T(8,128)(2,1)}, u32[]{:S(2)}) copy-start(bf16[256,64]{0,1:T(8,128)(2,1)} %param.27) | copy-start | bytes 98308
  17.0 1.1 %copy-start.16 = (f32[256]{0:T(256)S(1)}, f32[256]{0:T(256)}, u32[]{:S(2)}) copy-start(f32[256]{0:T(256)} %param.26) | copy-start | bytes 3076
  17.1 1.1 %copy-start.17 = (f32[256]{0:T(256)S(1)}, f32[256]{0:T(256)}, u32[]{:S(2)}) copy-start(f32[256]{0:T(256)} %param.25) | copy-start | bytes 3076
  20.4 14.7 %all-to-all-start = ((bf16[4,16,128,65]{2,1,3,0:T(8,128)(2,1)}), bf16[4,16,128,65]{2,1,3,0:T(8,128)(2,1)S(1)}, u32[]{:S(2)}, u32[]{:S(2)}) async-start(bf16[4,16,128,65]{2,1,3,0:T(8,128)(2,1)} %broadcast_in_dim.8), calls=%async_computation | async-start | bytes 2129920 | tf_op jit(solution)/shard_map/all_to_all | solution.py:11
  35.4 2.7 %copy-start.7 = (f32[128]{0:T(128)S(1)}, f32[128]{0:T(128)}, u32[]{:S(2)}) copy-start(f32[128]{0:T(128)} %param.29) | copy-start | bytes 1540
  81.1 6.9 %copy-start.3 = (bf16[32,128,128]{2,1,0:T(8,128)(2,1)S(1)}, bf16[32,128,128]{2,1,0:T(8,128)(2,1)}, u32[]{:S(2)}) copy-start(bf16[32,128,128]{2,1,0:T(8,128)(2,1)} %get-tuple-element.66) | copy-start | bytes 3145732 | tf_op jit(solution)/shard_map/cond
  93.4 1.3 %copy-start.9 = (f32[128]{0:T(128)S(1)}, f32[128]{0:T(128)}, u32[]{:S(2)}) copy-start(f32[128]{0:T(128)} %param.35) | copy-start | bytes 1540
  93.4 1.4 %copy-start.10 = (f32[128]{0:T(128)S(1)}, f32[128]{0:T(128)}, u32[]{:S(2)}) copy-start(f32[128]{0:T(128)} %param.34) | copy-start | bytes 1540
  94.1 1.7 %copy-start.13 = (bf16[4,8,64,128]{3,2,1,0:T(8,128)(2,1)S(1)}, bf16[4,8,64,128]{3,2,1,0:T(8,128)(2,1)}, u32[]{:S(2)}) copy-start(bf16[4,8,64,128]{3,2,1,0:T(8,128)(2,1)} %get-tuple-element.51) | copy-start | bytes 1572868
  94.7 1.3 %copy-start.2 = (bf16[32,128,128]{2,1,0:T(8,128)(2,1)S(1)}, bf16[32,128,128]{2,1,0:T(8,128)(2,1)}, u32[]{:S(2)}) copy-start(bf16[32,128,128]{2,1,0:T(8,128)(2,1)} %param.23) | copy-start | bytes 3145732
  94.7 1.9 %copy-start.5 = (f32[32,128,128]{2,1,0:T(8,128)S(1)}, f32[32,128,128]{2,1,0:T(8,128)}, u32[]{:S(2)}) copy-start(f32[32,128,128]{2,1,0:T(8,128)} %get-tuple-element.85) | copy-start | bytes 6291460
  94.7 1.9 %copy-start.15 = (bf16[128,128]{1,0:T(8,128)(2,1)S(1)}, bf16[128,128]{1,0:T(8,128)(2,1)}, u32[]{:S(2)}) copy-start(bf16[128,128]{1,0:T(8,128)(2,1)} %param.36) | copy-start | bytes 98308
  94.7 1.9 %copy-start.18 = (f32[128]{0:T(128)S(1)}, f32[128]{0:T(128)}, u32[]{:S(2)}) copy-start(f32[128]{0:T(128)} %param.37) | copy-start | bytes 1540
Sparse Core Ops, SparseCore 0:
  17.2 63.8 all-gather.1
where the time goes:
time: 106 us; the launch traced here: 105 us
  waiting for transfers between devices  26.8 us (25%)
  local copies, waits for them, and re-layouts  25.9 us (24%)
  matrix products  21.6 us (20%)
  between operations  13.7 us (13%)
  other arithmetic  12 us (11%)
  starting transfers between devices  4.88 us (5%)
    all_gather x1, waiting for transfers between devices, local(): incoming = lax.all_gather(right_own, 'dap', axis=0, tiled=True)  16.9 us
    all_to_all x1, waiting for transfers between devices, from_everyone(): return lax.all_to_all(copies, axis, split_axis=0, concat_axis=0, tiled=True)  9.83 us
    another operation x2, local copies, waits for them, and re-layouts  7.83 us
    dot_general x4, matrix products, one_block(): jnp.einsum('sic,sjd->ijcd', left_block, right_cols, preferred_element_typ...  7.11 us
    dot_general x4, matrix products, one_block(): jnp.dot(flat, pairwise_final_matrix, preferred_element_type=jnp.float32)  5.74 us
    convert_element_type x4, local copies, waits for them, and re-layouts, one_block(): averaged = (products * inverse_block[:, :, None, None]).astype(jnp.bfloat16)  5.42 us
    reshape x4, local copies, waits for them, and re-layouts, one_block(): flat = averaged.reshape(block_rows * columns, width_c * width_c)  5.04 us
    all_to_all x1, starting transfers between devices, from_everyone(): return lax.all_to_all(copies, axis, split_axis=0, concat_axis=0, tiled=True)  4.84 us
  transfers between devices with their start and end apart: 2, of which 2 were waited for; matrix products, arithmetic and copies ran while one was open for 31% of the time, Pallas kernels for 0%

commit v1 on v0

v1 whole, which is shorter than its diff:
```python
import jax
import jax.numpy as jnp
from jax import lax
from jax.experimental import pallas as pl
from jax.experimental.pallas import tpu as pltpu
from jax.sharding import PartitionSpec as P

F32 = jnp.float32
BF16 = jnp.bfloat16
EPS = 1e-05
NT = (((1,), (1,)), ((), ()))
VMEM = pl.BlockSpec(memory_space=pltpu.VMEM)
SMEM = pl.BlockSpec(memory_space=pltpu.SMEM)


def dot(a, b):
    return jnp.dot(a, b, preferred_element_type=F32)


def dot_nt(a, b):
    return lax.dot_general(a, b, NT, preferred_element_type=F32)


def sigmoid(v):
    return 0.5 * jnp.tanh(0.5 * v) + 0.5


def flipped(a):
    return jnp.transpose(a.astype(F32))


def column(row, width):
    return jnp.transpose(jnp.broadcast_to(row, (width, row.shape[1])))


def normed(x, gain, bias, ones):
    width = x.shape[1]
    tiles = width // 128
    mean = dot(x, ones[:width])
    mean = mean if tiles == 1 else jnp.concatenate([mean] * tiles, axis=1)
    delta = x.astype(F32) - mean
    square = delta * delta
    high = square.astype(BF16)
    low = (square - high.astype(F32)).astype(BF16)
    spread = dot(jnp.concatenate([high, low], axis=1), ones)
    scale = lax.rsqrt(spread + EPS)
    scale = scale if tiles == 1 else jnp.concatenate([scale] * tiles, axis=1)
    return (delta * scale * gain + bias).astype(BF16)


def msa_kernel(place, x_ref, flag_ref, window_ref, gain_ref, bias_ref, w_ref, *outs):
    d, b = place[0], place[1]
    seqs, residues, width = x_ref.shape
    ones = jnp.full((2 * width, 128), 1.0 / width, BF16)
    wt = flipped(w_ref[...]).astype(BF16)
    gain, bias = gain_ref[...], bias_ref[...]
    live_all = flag_ref[...].astype(F32) * window_ref[...].astype(F32)
    lane = lax.broadcasted_iota(jnp.int32, (8, 128), 1)
    lane16 = lax.broadcasted_iota(jnp.int32, (16, 128), 1)
    first = b == 0

    for s in range(seqs):
        xn = normed(x_ref[s], gain, bias, ones)
        projected = dot_nt(wt, xn)
        live = jnp.broadcast_to(live_all[s : s + 1, :], (8, 128))
        left = [projected[q * 8 : q * 8 + 8] * live for q in range(4)]
        live16 = jnp.concatenate([live, live], axis=0)
        lo = projected[32:48] * live16
        hi = projected[48:64] * live16
        same = jnp.where(lane16 < 64, lo, hi)
        right = jnp.where(
            first,
            jnp.where(lane16 < 64, lo, pltpu.roll(hi, 64, 1)),
            jnp.where(lane16 < 64, pltpu.roll(lo, 64, 1), hi),
        )
        live_cols = jnp.where(first, pltpu.roll(live, 32, 1), pltpu.roll(live, 96, 1))
        for r in range(4):
            dest = lax.rem(d + r, 4)
            merged = jnp.zeros((8, 128), F32)
            for q in range(4):
                turned = pltpu.roll(left[q], lax.rem(32 * (q - dest) + 128, 128), 1)
                merged = jnp.where((lane >= 32 * q) & (lane < 32 * q + 32), turned, merged)
            live_rows = pltpu.roll(live, lax.rem(128 - 32 * dest, 128), 1)
            flags = jnp.where(lane < 32, live_rows, live_cols)
            outs[r][s] = jnp.concatenate([merged, right, flags], axis=0).astype(BF16)


def pair_kernel(
    place, x_ref, window_ref, gain_ref, bias_ref, w_ref, wb_ref, wf_ref,
    left_ref, gate_ref, wcat_ref, scr, xn_scr, wf_scr,
):
    d, b = place[0], place[1]
    rows, residues, width = x_ref.shape
    ones = jnp.full((2 * width, 128), 1.0 / width, BF16)
    gain, bias = gain_ref[...], bias_ref[...]
    wt = flipped(w_ref[:, 0:256]).astype(BF16)
    wg = flipped(w_ref[:, 512:640]).astype(BF16)
    wcol = column(wb_ref[:, 0:256], 128)
    gcol = column(wb_ref[:, 512:640], 128)
    live_k = window_ref[...].astype(F32)

    wf_scr[...] = wf_ref[...].astype(F32)
    for p in range(2):
        for t in range(4):
            parts = [wf_scr[pl.ds(p * 16 + 4 * t + u, 32, stride=32), :] for u in range(4)]
            block = jnp.transpose(jnp.concatenate(parts, axis=0))
            wcat_ref[128 * p : 128 * p + 128, 128 * t : 128 * t + 128] = block.astype(BF16)

    def one(i, _):
        xn = normed(x_ref[i], gain, bias, ones)
        xn_scr[i] = xn
        projected = dot_nt(wt, xn) + wcol
        live = live_k * place[2 + d * rows + i].astype(F32)
        scr[pl.ds(i * 128, 128), :] = sigmoid(projected[0:128]) * projected[128:256] * live
        return 0

    lax.fori_loop(0, rows, one, 0, unroll=4)

    def gates(p, _):
        at = pl.multiple_of(64 * b, 64)
        both = jnp.concatenate(
            [xn_scr[p, pl.ds(at, 64), :], xn_scr[p + rows // 2, pl.ds(at, 64), :]], axis=0
        )
        gate_ref[p] = sigmoid(dot_nt(wg, both) + gcol)
        return 0

    lax.fori_loop(0, rows // 2, gates, 0, unroll=4)

    def turn(c, _):
        left_ref[c] = scr[pl.ds(c, rows, stride=128), :].astype(BF16)
        return 0

    lax.fori_loop(0, 128, turn, 0, unroll=8)


def outer_kernel(m0, m1, m2, m3, wcat_ref, fb_ref, out_ref, m_scr, a_scr, r_scr, inv_scr, s_scr):
    for r, m in enumerate((m0, m1, m2, m3)):
        m_scr[pl.ds(r * 512, 512), :] = m[...].reshape(512, 128).astype(F32)

    def row(k):
        return m_scr[pl.ds(k, 64, stride=32), :]

    flags = row(24)
    count = dot(jnp.transpose(flags).astype(BF16), flags.astype(BF16))[0:32]
    inverse = 1.0 / jnp.maximum(count, 1.0)
    lane = lax.broadcasted_iota(jnp.int32, (16, 128), 1)
    inv_scr[...] = jnp.where(
        lane < 64, pltpu.roll(inverse[0:16], 96, 1), pltpu.roll(inverse[16:32], 32, 1)
    )
    for r in range(8):
        turned = jnp.transpose(row(r))
        for q in range(4):
            a_scr[pl.ds((q * 8 + r) * 32, 32), :] = turned[32 * q : 32 * q + 32]
    for t in range(16):
        r_scr[:, 128 * t : 128 * t + 128] = row(8 + t).astype(BF16)

    wcat = wcat_ref[...]
    bcol = column(fb_ref[...], 128)
    lane2 = lax.broadcasted_iota(jnp.int32, (128, 128), 1)

    def one(p, _):
        a = jnp.concatenate(
            [a_scr[pl.ds(p, 32, stride=32), :], a_scr[pl.ds(p + 16, 32, stride=32), :]], axis=0
        ).astype(BF16)
        products = dot(a, r_scr[...]).astype(BF16)
        stacked = [
            jnp.concatenate(
                [products[0:32, 128 * t : 128 * t + 128], products[32:64, 128 * t : 128 * t + 128]],
                axis=1,
            )
            for t in range(16)
        ]
        update = dot(wcat, jnp.concatenate(stacked, axis=0))
        a0, a1 = update[0:128, 0:128], update[0:128, 128:256]
        b0, b1 = update[128:256, 0:128], update[128:256, 128:256]
        total = jnp.where(lane2 < 64, a0, b1) + pltpu.roll(jnp.where(lane2 < 64, a1, b0), 64, 1)
        out_ref[p] = (total * inv_scr[pl.ds(p, 1), :] + bcol).astype(BF16)
        return 0

    lax.fori_loop(0, 16, one, 0, unroll=2)


def triangle_kernel(
    place, own_ref, far_a, far_b, near_d, window_ref, gain_ref, bias_ref, w_ref, wb_ref,
    left_ref, gate_ref, opm_ref, fg_ref, fo_ref, wt_ref, tb_ref,
    out_ref, r_scr, t_scr,
):
    d, b = place[0], place[1]
    rows, residues, width = own_ref.shape
    member = (d // 2) == b
    ones = jnp.full((2 * width, 128), 1.0 / width, BF16)
    gain, bias = gain_ref[...], bias_ref[...]
    wt = flipped(w_ref[:, 256:512]).astype(BF16)
    wcol = column(wb_ref[:, 256:512], 128)
    live_k = window_ref[...].astype(F32)
    odd = lax.rem(d, 2)

    def project(x, slot, j):
        xn = normed(x, gain, bias, ones)
        projected = dot_nt(wt, xn) + wcol
        at = slot * rows + j
        live = live_k * place[2 + 64 * b + at].astype(F32)
        r_scr[pl.ds(at * 128, 128), :] = sigmoid(projected[0:128]) * projected[128:256] * live

    def one_row(j, _):
        project(jnp.where(member, own_ref[j], near_d[j]), odd, j)
        project(jnp.where(member, far_a[j], far_b[j]), 1 - odd, j)
        return 0

    lax.fori_loop(0, rows, one_row, 0, unroll=2)

    lane = lax.broadcasted_iota(jnp.int32, (16, 128), 1)

    def channel(c, _):
        right = r_scr[pl.ds(c, 64, stride=128), :].astype(BF16)
        prod = dot_nt(left_ref[c], jnp.concatenate([right, right], axis=0))
        t_scr[pl.ds(c * 16, 16), :] = jnp.where(lane < 64, prod[0:16], prod[16:32])
        return 0

    lax.fori_loop(0, 128, channel, 0, unroll=8)

    fg = column(fg_ref[...], 128)
    fo = column(fo_ref[...], 128)
    tb = column(tb_ref[...], 128)
    final = flipped(wt_ref[...]).astype(BF16)

    def finish(p, _):
        x = t_scr[pl.ds(p, 128, stride=16), :]
        mean = jnp.sum(x, axis=0, keepdims=True) * (1.0 / 128)
        delta = x - mean
        spread = jnp.sum(delta * delta, axis=0, keepdims=True) * (1.0 / 128)
        mid = (delta * lax.rsqrt(spread + EPS) * fg + fo).astype(BF16)
        update = (gate_ref[p] * (dot(final, mid) + tb)).astype(BF16)
        total = jnp.transpose(update.astype(F32) + opm_ref[p].astype(F32))
        at = pl.multiple_of(64 * b, 64)
        for h in range(2):
            i = p + h * (rows // 2)
            base = own_ref[i, pl.ds(at, 64), :].astype(F32)
            out_ref[i] = (base + total[64 * h : 64 * h + 64]).astype(BF16)
        return 0

    lax.fori_loop(0, rows // 2, finish, 0, unroll=2)


def call(kernel, shapes, ins, scratch=(), cost=None):
    return pl.pallas_call(
        kernel,
        out_shape=shapes,
        in_specs=ins,
        out_specs=jax.tree.map(lambda _: VMEM, shapes),
        scratch_shapes=list(scratch),
        compiler_params=pltpu.CompilerParams(vmem_limit_bytes=40 * 1024 * 1024),
        cost_estimate=cost,
    )


SDS = jax.ShapeDtypeStruct


def local(
    homolog_matrix,
    homolog_entry_flags,
    couple_matrix,
    window_amino_flags,
    pairwise_standardize_scaling,
    pairwise_standardize_offset,
    pairwise_factor_matrices,
    pairwise_final_matrix,
    pairwise_final_offset,
    trimul_entry_standardize_scaling,
    trimul_entry_standardize_offset,
    trimul_entry_matrices,
    trimul_entry_offsets,
    trimul_final_standardize_scaling,
    trimul_final_standardize_offset,
    trimul_final_matrix,
    trimul_final_offset,
):
    d, b = lax.axis_index("dap"), lax.axis_index("branch")
    rows, residues, width = couple_matrix.shape
    place = jnp.concatenate([jnp.stack([d, b]).astype(jnp.int32), window_amino_flags])
    window = window_amino_flags[None, :]
    both = ("branch", "dap")

    swap = [(0, 1), (1, 0), (7, 6), (6, 7)]
    across = [(0, 3), (1, 2), (7, 4), (6, 5)]
    around = [(4, 2), (5, 3), (3, 5), (2, 4)]
    far_a = lax.ppermute(couple_matrix, both, swap)
    far_b = lax.ppermute(couple_matrix, both, across)
    near_d = lax.ppermute(couple_matrix, both, around)

    seqs = homolog_matrix.shape[0]
    message = SDS((seqs, 32, 128), BF16)
    parts = call(
        msa_kernel, [message] * 4, [SMEM] + [VMEM] * 6,
        cost=pl.CostEstimate(flops=100_000_000, bytes_accessed=2_000_000, transcendentals=0),
    )(
        place, homolog_matrix, homolog_entry_flags, window,
        pairwise_standardize_scaling[None], pairwise_standardize_offset[None],
        pairwise_factor_matrices,
    )
    arrived = [parts[0]] + [
        lax.ppermute(parts[r], "dap", [(k, (k + r) % 4) for k in range(4)]) for r in (1, 2, 3)
    ]

    left, gate, wcat = call(
        pair_kernel,
        [
            SDS((128, rows, 128), BF16),
            SDS((rows // 2, 128, 128), F32),
            SDS((256, 512), BF16),
        ],
        [SMEM] + [VMEM] * 7,
        [
            pltpu.VMEM((rows * 128, 128), F32),
            pltpu.VMEM((rows, 128, 128), BF16),
            pltpu.VMEM((1024, 128), F32),
        ],
        cost=pl.CostEstimate(flops=600_000_000, bytes_accessed=4_000_000, transcendentals=0),
    )(
        place, couple_matrix, window,
        trimul_entry_standardize_scaling[None], trimul_entry_standardize_offset[None],
        trimul_entry_matrices, trimul_entry_offsets[None], pairwise_final_matrix,
    )

    opm = call(
        outer_kernel,
        SDS((rows // 2, 128, 128), BF16),
        [VMEM] * 6,
        [
            pltpu.VMEM((2048, 128), F32),
            pltpu.VMEM((1024, 64), F32),
            pltpu.VMEM((64, 2048), BF16),
            pltpu.VMEM((16, 128), F32),
            pltpu.VMEM((8, 128), F32),
        ],
        cost=pl.CostEstimate(flops=1_600_000_000, bytes_accessed=2_000_000, transcendentals=0),
    )(*arrived, wcat, pairwise_final_offset[None])

    return call(
        triangle_kernel,
        SDS((rows, 64, 128), BF16),
        [SMEM] + [VMEM] * 16,
        [pltpu.VMEM((64 * 128, 128), F32), pltpu.VMEM((128 * 16, 128), F32)],
    )(
        place, couple_matrix, far_a, far_b, near_d, window,
        trimul_entry_standardize_scaling[None], trimul_entry_standardize_offset[None],
        trimul_entry_matrices, trimul_entry_offsets[None],
        left, gate, opm,
        trimul_final_standardize_scaling[None], trimul_final_standardize_offset[None],
        trimul_final_matrix, trimul_final_offset[None],
    )


def solution(mesh):
    placed = (
        P(("crop", "dap"), None, None),
        P(("crop", "dap"), None),
        P(("crop", "dap"), None, None),
        P("crop"),
    ) + (P(),) * 13
    return jax.shard_map(
        local,
        mesh=mesh,
        in_specs=placed,
        out_specs=P(("crop", "dap"), "branch", None),
        check_vma=False,
    )
```

time: 106 us -> 107 us (level)
  the two profiles are of different devices: /device:TPU:1 before, /device:TPU:690 now
where the time goes in v1:
time: 107 us
  starting transfers between devices  51.1 us (48%)
  Pallas kernels  48.4 us (45%)
  local copies, waits for them, and re-layouts  6.64 us (6%)
    ppermute x3, starting transfers between devices, local(): lax.ppermute(parts[r], 'dap', [(k, (k + r) % 4) for k in range(4)])  43.7 us
    pallas_call x1, Pallas kernels, local(): call(triangle_kernel, SDS((rows, 64, 128), BF16), [SMEM] + [VMEM] * 16, [...  24.6 us
    pallas_call x1, Pallas kernels, local(): call(pair_kernel, [SDS((128, rows, 128), BF16), SDS((rows // 2, 128, 128)...  11 us
    pallas_call x1, Pallas kernels, local(): call(outer_kernel, SDS((rows // 2, 128, 128), BF16), [VMEM] * 6, [pltpu.V...  6.98 us
    unnamed x33, local copies, waits for them, and re-layouts  6.64 us
    pallas_call x1, Pallas kernels, local(): call(msa_kernel, [message] * 4, [SMEM] + [VMEM] * 6, cost=pl.CostEstimate...  5.81 us
    ppermute x1, starting transfers between devices, local(): near_d = lax.ppermute(couple_matrix, both, around)  5.38 us
  transfers between devices with their start and end apart: 6, of which 1 were waited for; matrix products, arithmetic and copies ran while one was open for 1% of the time, Pallas kernels for 22%

profile of v1, /device:TPU:690, one launch (start us, length us, event | category | flops | bytes accessed | tf_op | source)
XLA Modules:
  0.0 107.0 jit_solution(1258241458214355654)
XLA Ops:
  0.0 0.7 collective-permute-start
  0.7 1.3 %collective-permute-start.1 = (bf16[32,128,128]{2,1,0:T(8,128)(2,1)}, bf16[32,128,128]{2,1,0:T(8,128)(2,1)S(1)}, u32[]{:S(2)}, u32[]{:S(2)}) collective-permute-start(bf16[32,128,128]{2,1,0:T(8,128)(2,1)} %own_ref.1), channel_id=1, source_target_pairs={{0,3},{1,2},{7,4},{6,5},{8,11},{9,10},{15,12},{14,13},{16,19},{17,... | collective-permute-start | bytes 3145736 | tf_op jit(solution)/shard_map/ppermute | solution.py:289
  2.0 5.4 %collective-permute-start.2 = (bf16[32,128,128]{2,1,0:T(8,128)(2,1)}, bf16[32,128,128]{2,1,0:T(8,128)(2,1)S(1)}, u32[]{:S(2)}, u32[]{:S(2)}) collective-permute-start(bf16[32,128,128]{2,1,0:T(8,128)(2,1)} %own_ref.1), channel_id=1, source_target_pairs={{4,2},{5,3},{3,5},{2,4},{12,10},{13,11},{11,13},{10,12},{20,18},{2... | collective-permute-start | bytes 3145736 | tf_op jit(solution)/shard_map/ppermute | solution.py:290
  7.4 0.0 copy-start.5
  7.4 0.9 copy.18.w_ref
  8.3 0.0 copy-start.4
  8.3 0.0 copy-done.5
  8.3 0.1 pad_add_fusion.place
  8.4 0.0 copy-start.7
  8.4 0.0 copy-start.6
  8.4 0.6 copy-done.4
  9.0 0.1 copy-done.7
  9.1 0.0 copy-done.6
  9.1 0.0 copy-start
  9.1 1.2 %copy-done = bf16[16,128,256]{2,1,0:T(8,128)(2,1)S(1)} copy-done((bf16[16,128,256]{2,1,0:T(8,128)(2,1)S(1)}, bf16[16,128,256]{2,1,0:T(8,128)(2,1)}, u32[]{:S(2)}) %copy-start) | copy-done | bytes 1048600
  10.3 0.0 copy-start.1
  10.3 5.8 %shard_map.164 = (bf16[16,32,128]{2,1,0:T(8,128)(2,1)S(1)}, bf16[16,32,128]{2,1,0:T(8,128)(2,1)S(1)}, bf16[16,32,128]{2,1,0:T(8,128)(2,1)S(1)}, bf16[16,32,128]{2,1,0:T(8,128)(2,1)S(1)}) custom-call(s32[130]{0:T(256)S(1)} %pad_add_fusion.place, bf16[16,128,256]{2,1,0:T(8,128)(2,1)S(1)} %copy-done, s32[16,128]{1,0:T(8,128)S(1)} %copy-done.4, ...), custom_call_target="tpu_custom_call" | custom-call | flops 100000000 | bytes 2000000 | tf_op jit(solution)/shard_map/pallas_call | solution.py:294
  16.2 0.0 copy-start.15
  16.2 1.9 %collective-permute-start.3 = (bf16[16,32,128]{2,1,0:T(8,128)(2,1)S(1)}, bf16[16,32,128]{2,1,0:T(8,128)(2,1)S(1)}, u32[]{:S(2)}, u32[]{:S(2)}) collective-permute-start(bf16[16,32,128]{2,1,0:T(8,128)(2,1)S(1)} %get-tuple-element.15), channel_id=1, source_target_pairs={{0,1},{1,2},{2,3},{3,0},{4,5},{5,6},{6,7},{7,4},{8,9},{9,10},{10,1... | collective-permute-start | bytes 393224 | tf_op jit(solution)/shard_map/ppermute | solution.py:303
  18.1 5.4 %collective-permute-start.4 = (bf16[16,32,128]{2,1,0:T(8,128)(2,1)S(1)}, bf16[16,32,128]{2,1,0:T(8,128)(2,1)S(1)}, u32[]{:S(2)}, u32[]{:S(2)}) collective-permute-start(bf16[16,32,128]{2,1,0:T(8,128)(2,1)S(1)} %get-tuple-element.16), channel_id=1, source_target_pairs={{0,2},{1,3},{2,0},{3,1},{4,6},{5,7},{6,4},{7,5},{8,10},{9,11},{10,... | collective-permute-start | bytes 393224 | tf_op jit(solution)/shard_map/ppermute | solution.py:303
  23.5 0.5 collective-permute-done.3.m1
  24.0 36.4 %collective-permute-start.5 = (bf16[16,32,128]{2,1,0:T(8,128)(2,1)S(1)}, bf16[16,32,128]{2,1,0:T(8,128)(2,1)S(1)}, u32[]{:S(2)}, u32[]{:S(2)}) collective-permute-start(bf16[16,32,128]{2,1,0:T(8,128)(2,1)S(1)} %get-tuple-element.17), channel_id=1, source_target_pairs={{0,3},{1,0},{2,1},{3,2},{4,7},{5,4},{6,5},{7,6},{8,11},{9,8},{10,9... | collective-permute-start | bytes 393224 | tf_op jit(solution)/shard_map/ppermute | solution.py:303
  60.4 0.0 copy-done.15
  60.4 0.0 copy-start.8
  60.4 0.0 copy-start.9
  60.4 0.0 copy-done.1
  60.4 0.6 copy-done.8
  61.1 0.0 copy-done.9
  61.1 0.0 copy-start.2
  61.1 0.9 copy-done.2
  62.0 0.9 copy-done.13
  63.0 11.0 %shard_map.163 = (bf16[128,32,128]{2,1,0:T(8,128)(2,1)S(1)}, f32[16,128,128]{2,1,0:T(8,128)S(1)}, bf16[256,512]{1,0:T(8,128)(2,1)S(1)}) custom-call(s32[130]{0:T(256)S(1)} %pad_add_fusion.place, bf16[32,128,128]{2,1,0:T(8,128)(2,1)S(1)} %copy-done.1, s32[1,128]{1,0:T(1,128)S(1)} %bitcast.12, f32[1,128]{1,0:T(1,128)S(1)} %bitcast.16, f32[1,128]{1,0:T(1,128)S(1)} %bitcast.18, ...), custom_call_target="tpu_custom_call" | custom-call | flops 600000000 | bytes 4000000 | tf_op jit(solution)/shard_map/pallas_call | solution.py:306
  74.0 0.0 collective-permute-done.4.m2
  74.0 0.0 collective-permute-done.5.m3
  74.0 0.0 copy-start.14
  74.0 0.6 copy-done.14
  74.6 7.0 %shard_map.165.opm_ref = bf16[16,128,128]{2,1,0:T(8,128)(2,1)S(1)} custom-call(bf16[16,32,128]{2,1,0:T(8,128)(2,1)S(1)} %get-tuple-element.14.m0, bf16[16,32,128]{2,1,0:T(8,128)(2,1)S(1)} %collective-permute-done.3.m1, bf16[16,32,128]{2,1,0:T(8,128)(2,1)S(1)} %collective-permute-done.4.m2, bf16[16,32,128]{2,1,0:T(8,128)(2,1)S(1)} %collective-permute-done.5.m3, ...), custom_call_target="tpu_custom_call" | custom-call | flops 1600000000 | bytes 2000000 | tf_op jit(solution)/shard_map/pallas_call | solution.py:326
  81.6 0.0 collective-permute-done.far_a
  81.6 0.0 collective-permute-done.1.far_b
  81.6 0.0 collective-permute-done.2.near_d
  81.7 0.0 copy-start.10
  81.7 0.0 copy-start.11
  81.7 0.0 copy-start.12
  81.7 0.0 copy-done.3
  81.7 0.6 copy-done.10
  82.3 0.0 copy-done.11
  82.3 0.0 copy-done.12
  82.3 24.6 %shard_map.166 = bf16[32,64,128]{2,1,0:T(8,128)(2,1)} custom-call(s32[130]{0:T(256)S(1)} %pad_add_fusion.place, bf16[32,128,128]{2,1,0:T(8,128)(2,1)S(1)} %copy-done.1, bf16[32,128,128]{2,1,0:T(8,128)(2,1)S(1)} %collective-permute-done.far_a, bf16[32,128,128]{2,1,0:T(8,128)(2,1)S(1)} %collective-permute-done.1.far_b, ...), custom_call_target="tpu_custom_call" | custom-call | tf_op jit(solution)/shard_map/pallas_call | solution.py:340
  (3 shorter events, 0.0 us)
Async XLA Ops:
  0.0 81.6 %collective-permute-start = (bf16[32,128,128]{2,1,0:T(8,128)(2,1)}, bf16[32,128,128]{2,1,0:T(8,128)(2,1)S(1)}, u32[]{:S(2)}, u32[]{:S(2)}) collective-permute-start(bf16[32,128,128]{2,1,0:T(8,128)(2,1)} %own_ref.1), channel_id=1, source_target_pairs={{0,1},{1,0},{7,6},{6,7},{8,9},{9,8},{15,14},{14,15},{16,17},{17,16... | collective-permute-start | bytes 3145736 | tf_op jit(solution)/shard_map/ppermute | solution.py:288
  0.7 80.9 %collective-permute-start.1 = (bf16[32,128,128]{2,1,0:T(8,128)(2,1)}, bf16[32,128,128]{2,1,0:T(8,128)(2,1)S(1)}, u32[]{:S(2)}, u32[]{:S(2)}) collective-permute-start(bf16[32,128,128]{2,1,0:T(8,128)(2,1)} %own_ref.1), channel_id=1, source_target_pairs={{0,3},{1,2},{7,4},{6,5},{8,11},{9,10},{15,12},{14,13},{16,19},{17,... | collective-permute-start | bytes 3145736 | tf_op jit(solution)/shard_map/ppermute | solution.py:289
  2.0 79.6 %collective-permute-start.2 = (bf16[32,128,128]{2,1,0:T(8,128)(2,1)}, bf16[32,128,128]{2,1,0:T(8,128)(2,1)S(1)}, u32[]{:S(2)}, u32[]{:S(2)}) collective-permute-start(bf16[32,128,128]{2,1,0:T(8,128)(2,1)} %own_ref.1), channel_id=1, source_target_pairs={{4,2},{5,3},{3,5},{2,4},{12,10},{13,11},{11,13},{10,12},{20,18},{2... | collective-permute-start | bytes 3145736 | tf_op jit(solution)/shard_map/ppermute | solution.py:290
  7.4 0.9 copy-start.5
  8.3 0.7 copy-start.4
  8.4 0.7 copy-start.7
  8.4 0.7 copy-start.6
  9.1 1.2 %copy-start = (bf16[16,128,256]{2,1,0:T(8,128)(2,1)S(1)}, bf16[16,128,256]{2,1,0:T(8,128)(2,1)}, u32[]{:S(2)}) copy-start(bf16[16,128,256]{2,1,0:T(8,128)(2,1)} %x_ref.3) | copy-start | bytes 3145732
  10.3 50.1 %copy-start.1 = (bf16[32,128,128]{2,1,0:T(8,128)(2,1)S(1)}, bf16[32,128,128]{2,1,0:T(8,128)(2,1)}, u32[]{:S(2)}) copy-start(bf16[32,128,128]{2,1,0:T(8,128)(2,1)} %own_ref.1) | copy-start | bytes 3145732
  16.2 44.2 %copy-start.15 = (f32[640]{0:T(1024)S(1)}, f32[640]{0:T(1024)}, u32[]{:S(2)}) copy-start(f32[640]{0:T(1024)} %param.29) | copy-start | bytes 7684
  16.2 7.8 %collective-permute-start.3 = (bf16[16,32,128]{2,1,0:T(8,128)(2,1)S(1)}, bf16[16,32,128]{2,1,0:T(8,128)(2,1)S(1)}, u32[]{:S(2)}, u32[]{:S(2)}) collective-permute-start(bf16[16,32,128]{2,1,0:T(8,128)(2,1)S(1)} %get-tuple-element.15), channel_id=1, source_target_pairs={{0,1},{1,2},{2,3},{3,0},{4,5},{5,6},{6,7},{7,4},{8,9},{9,10},{10,1... | collective-permute-start | bytes 393224 | tf_op jit(solution)/shard_map/ppermute | solution.py:303
  18.1 55.9 %collective-permute-start.4 = (bf16[16,32,128]{2,1,0:T(8,128)(2,1)S(1)}, bf16[16,32,128]{2,1,0:T(8,128)(2,1)S(1)}, u32[]{:S(2)}, u32[]{:S(2)}) collective-permute-start(bf16[16,32,128]{2,1,0:T(8,128)(2,1)S(1)} %get-tuple-element.16), channel_id=1, source_target_pairs={{0,2},{1,3},{2,0},{3,1},{4,6},{5,7},{6,4},{7,5},{8,10},{9,11},{10,... | collective-permute-start | bytes 393224 | tf_op jit(solution)/shard_map/ppermute | solution.py:303
  24.0 50.0 %collective-permute-start.5 = (bf16[16,32,128]{2,1,0:T(8,128)(2,1)S(1)}, bf16[16,32,128]{2,1,0:T(8,128)(2,1)S(1)}, u32[]{:S(2)}, u32[]{:S(2)}) collective-permute-start(bf16[16,32,128]{2,1,0:T(8,128)(2,1)S(1)} %get-tuple-element.17), channel_id=1, source_target_pairs={{0,3},{1,0},{2,1},{3,2},{4,7},{5,4},{6,5},{7,6},{8,11},{9,8},{10,9... | collective-permute-start | bytes 393224 | tf_op jit(solution)/shard_map/ppermute | solution.py:303
  60.4 0.7 copy-start.8
  60.4 0.7 copy-start.9
  61.1 0.9 copy-start.2
  62.0 0.9 copy-start.13
  74.0 0.7 copy-start.14
  74.6 7.1 %copy-start.3 = (bf16[128,128]{1,0:T(8,128)(2,1)S(1)}, bf16[128,128]{1,0:T(8,128)(2,1)}, u32[]{:S(2)}) copy-start(bf16[128,128]{1,0:T(8,128)(2,1)} %wt_ref.1) | copy-start | bytes 98308
  81.7 0.7 copy-start.10
  81.7 0.7 copy-start.11
  81.7 0.7 copy-start.12

commit v2 on v1

v2 whole, which is shorter than its diff:
```python
import jax
import jax.numpy as jnp
from jax import lax
from jax.experimental import pallas as pl
from jax.experimental.pallas import tpu as pltpu
from jax.sharding import PartitionSpec as P

F32 = jnp.float32
BF16 = jnp.bfloat16
EPS = 1e-05
NT = (((1,), (1,)), ((), ()))
VMEM = pl.BlockSpec(memory_space=pltpu.VMEM)
SMEM = pl.BlockSpec(memory_space=pltpu.SMEM)
HBM = pl.BlockSpec(memory_space=pltpu.HBM)
ENTRY_MIB = 56
BLOCK = 16
PAIRS = 4


def dot(a, b):
    return jnp.dot(a, b, preferred_element_type=F32)


def dot_nt(a, b):
    return lax.dot_general(a, b, NT, preferred_element_type=F32)


def sigmoid(v):
    return 0.5 * jnp.tanh(0.5 * v) + 0.5


def flipped(a):
    return jnp.transpose(a.astype(F32))


def column(row, width):
    return jnp.transpose(jnp.broadcast_to(row, (width, row.shape[1])))


def centring(width, copies):
    n = width * copies
    r = lax.broadcasted_iota(jnp.int32, (n, n), 0)
    c = lax.broadcasted_iota(jnp.int32, (n, n), 1)
    inside = (r // width) == (c // width)
    value = jnp.where(r == c, 1.0 - 1.0 / width, -1.0 / width)
    return jnp.where(inside, value, 0.0).astype(BF16)


def deviations(blocks, centre, gain, ones):
    n = len(blocks)
    wide = [jnp.concatenate(blocks[i : i + 2], axis=1) for i in range(0, n, 2)]
    delta = dot(jnp.concatenate(wide, axis=0), centre)
    square = (delta * delta).astype(BF16)
    gained = (delta * jnp.concatenate([gain] * 2, axis=1)).astype(BF16)

    def stacked(a):
        parts = [a[64 * i : 64 * i + 128] if i % 2 == 0 else a[64 * i - 64 : 64 * i + 64] for i in range(n)]
        parts = [p[:, 128 * (i % 2) : 128 * (i % 2) + 128] for i, p in enumerate(parts)]
        return jnp.concatenate(parts, axis=0)

    spread = dot_nt(ones, stacked(square))
    return stacked(gained), lax.rsqrt(spread + EPS)[0:1]


def gate_weights(w_ref, wb_ref, bias, at):
    wt = flipped(w_ref[:, at : at + 256])
    shift = jnp.sum(wt * bias, axis=1, keepdims=True)
    col = column(wb_ref[:, at : at + 256], 128) + shift
    half = jnp.where(lax.broadcasted_iota(jnp.int32, (256, 128), 0) < 128, 0.5, 1.0)
    col = col * half
    return (wt * half).astype(BF16), jnp.concatenate([col, col], axis=1)


def gated(wt, col, gained, scale, live):
    projected = dot_nt(wt, gained) * scale + col
    value = projected[128:256] * live
    return jnp.tanh(projected[0:128]) * value + value


def project_rows(x_ref, present, at, rows, live_k, centre, gain, ones, sides):
    def some(u, _):
        i = BLOCK * u
        gained, scale = deviations([x_ref[i + h] for h in range(BLOCK)], centre, gain, ones)
        for v in range(0, BLOCK, 2):
            live = jnp.concatenate(
                [live_k * (0.5 * present[at + i + v + h].astype(F32)) for h in range(2)], axis=1
            )
            lanes = slice(128 * v, 128 * v + 256)
            for wt, col, scr in sides:
                result = gated(wt, col, gained[lanes], scale[:, lanes], live)
                for h in range(2):
                    scr[pl.ds((i + v + h) * 128, 128), :] = result[:, 128 * h : 128 * h + 128]
        return 0

    lax.fori_loop(0, rows // BLOCK, some, 0)


def msa_kernel(x_ref, flag_ref, window_ref, gain_ref, bias_ref, wt_ref, out_ref):
    b = lax.axis_index("branch")
    seqs, residues, width = x_ref.shape
    ones = jnp.full((8, width), 1.0 / width, BF16)
    centre = centring(width, 1)
    wt = wt_ref[...]
    col = jnp.sum(wt.astype(F32) * bias_ref[...], axis=1, keepdims=True)
    live_all = flag_ref[...].astype(F32) * window_ref[...].astype(F32)
    lane = lax.broadcasted_iota(jnp.int32, (8, 128), 1)
    lane16 = lax.broadcasted_iota(jnp.int32, (16, 128), 1)
    first = b == 0

    delta = dot(x_ref[...].reshape(seqs * residues, width), centre)
    spread = dot_nt(ones, (delta * delta).astype(BF16))
    gained = (delta * gain_ref[...]).astype(BF16)
    everything = dot_nt(wt, gained) * lax.rsqrt(spread + EPS)[0:1] + col
    for s in range(seqs):
        live_row = live_all[s : s + 1, :]
        projected = everything[:, 128 * s : 128 * s + 128] * live_row
        live = jnp.broadcast_to(live_row, (8, 128))
        lo, hi = projected[32:48], projected[48:64]
        right = jnp.where(
            first,
            jnp.where(lane16 < 64, lo, pltpu.roll(hi, 64, 1)),
            jnp.where(lane16 < 64, pltpu.roll(lo, 64, 1), hi),
        )
        live_cols = jnp.where(first, pltpu.roll(live, 32, 1), pltpu.roll(live, 96, 1))
        turned = [[projected[q * 8 : q * 8 + 8]] for q in range(4)]
        for q in range(4):
            turned[q] += [pltpu.roll(turned[q][0], 32 * k, 1) for k in range(1, 4)]
        for dest in range(4):
            merged = turned[0][-dest % 4]
            for q in range(1, 4):
                merged = jnp.where(lane >= 32 * q, turned[q][(q - dest) % 4], merged)
            live_rows = pltpu.roll(live, 128 - 32 * dest, 1) if dest else live
            flags = jnp.where(lane < 32, live_rows, live_cols)
            out_ref[dest, s] = jnp.concatenate([merged, right, flags], axis=0).astype(BF16)


def member_of_half():
    return (lax.axis_index("dap") // 2) == lax.axis_index("branch")


def sides_kernel(
    present, couple, window_ref, gain_ref, bias_ref, weight, offset,
    left_ref, right_ref, cross_ref, couple_v, weight_v, left_scr, right_scr, sems,
):
    rows = couple_v.shape[0]
    member = member_of_half()
    copies = [
        pltpu.make_async_copy(src, dst, sems.at[k])
        for k, (src, dst) in enumerate([(weight, weight_v), (couple, couple_v)])
    ]
    for copy in copies:
        copy.start()
    copies[0].wait()
    ones = jnp.full((8, 128), 1.0 / 128, BF16)
    bias = bias_ref[...]
    sides = [
        (*gate_weights(weight_v, offset, bias, 256 * k), scr)
        for k, scr in enumerate((left_scr, right_scr))
    ]
    copies[1].wait()
    live_k = window_ref[...].astype(F32)
    project_rows(
        couple_v, present, lax.axis_index("dap") * rows, rows, live_k,
        centring(128, 2), gain_ref[...], ones, sides,
    )

    def turn(c, _):
        left = [left_scr[pl.ds(c + 64 * h, rows, stride=128), :].astype(BF16) for h in range(2)]
        right = [right_scr[pl.ds(c + 64 * h, rows, stride=128), :].astype(BF16) for h in range(2)]
        for h in range(2):
            left_ref[c + 64 * h] = left[h]
            right_ref[c + 64 * h] = right[h]
        cross_ref[c] = jnp.where(member, right[1], left[0])
        return 0

    lax.fori_loop(0, 64, turn, 0, unroll=8)


def gate_kernel(
    x_ref, gain_ref, bias_ref, w_ref, wb_ref, wf_ref, gate_ref, wcat_ref, wf_scr,
):
    b = lax.axis_index("branch")
    rows = x_ref.shape[0]
    ones = jnp.full((8, 128), 1.0 / 128, BF16)
    centre, gain = centring(128, 2), gain_ref[...]
    wg = flipped(w_ref[:, 512:640])
    gcol = column(wb_ref[:, 512:640], 128) + jnp.sum(wg * bias_ref[...], axis=1, keepdims=True)
    wg, gcol = (0.5 * wg).astype(BF16), 0.5 * gcol
    at = pl.multiple_of(64 * b, 64)

    blocks = [
        jnp.concatenate([x_ref[p, pl.ds(at, 64), :], x_ref[p + rows // 2, pl.ds(at, 64), :]], axis=0)
        for p in range(rows // 2)
    ]
    gained, scale = deviations(blocks, centre, gain, ones)
    projected = dot_nt(wg, gained) * scale
    for p in range(rows // 2):
        part = projected[:, 128 * p : 128 * p + 128] + gcol
        gate_ref[p] = 0.5 * jnp.tanh(part) + 0.5

    wf_scr[...] = wf_ref[...].astype(F32)
    for p in range(2):
        for t in range(4):
            parts = [wf_scr[pl.ds(p * 16 + 4 * t + u, 32, stride=32), :] for u in range(4)]
            block = jnp.transpose(jnp.concatenate(parts, axis=0))
            wcat_ref[128 * p : 128 * p + 128, 128 * t : 128 * t + 128] = block.astype(BF16)


def outer_kernel(m_ref, wcat_ref, fb_ref, out_ref, m_scr, a_scr, r_scr, inv_scr):
    m_scr[...] = m_ref[...].reshape(2048, 128).astype(F32)

    def row(k):
        return m_scr[pl.ds(k, 64, stride=32), :]

    flags = row(24)
    count = dot(jnp.transpose(flags).astype(BF16), flags.astype(BF16))[0:32]
    inverse = 1.0 / jnp.maximum(count, 1.0)
    lane = lax.broadcasted_iota(jnp.int32, (16, 128), 1)
    inv_scr[...] = jnp.where(
        lane < 64, pltpu.roll(inverse[0:16], 96, 1), pltpu.roll(inverse[16:32], 32, 1)
    )
    for r in range(8):
        turned = jnp.transpose(row(r))
        for q in range(4):
            a_scr[pl.ds((q * 8 + r) * 32, 32), :] = turned[32 * q : 32 * q + 32]
    for t in range(16):
        r_scr[:, 128 * t : 128 * t + 128] = row(8 + t).astype(BF16)

    wcat = wcat_ref[...]
    bcol = column(fb_ref[...], 128)
    lane2 = lax.broadcasted_iota(jnp.int32, (128, 128), 1)

    def some(u, _):
        first = PAIRS * u
        a = [a_scr[pl.ds(first + p + 16 * h, 32, stride=32), :] for p in range(PAIRS) for h in range(2)]
        products = dot(jnp.concatenate(a, axis=0).astype(BF16), r_scr[...]).astype(BF16)
        for p in range(PAIRS):
            lo, hi = products[64 * p : 64 * p + 32], products[64 * p + 32 : 64 * p + 64]
            tiles = [slice(128 * t, 128 * t + 128) for t in range(16)]
            stacked = [jnp.concatenate([lo[:, t], hi[:, t]], axis=1) for t in tiles]
            update = dot(wcat, jnp.concatenate(stacked, axis=0))
            a0, a1 = update[0:128, 0:128], update[0:128, 128:256]
            b0, b1 = update[128:256, 0:128], update[128:256, 128:256]
            crossed = pltpu.roll(jnp.where(lane2 < 64, a1, b0), 64, 1)
            total = jnp.where(lane2 < 64, a0, b1) + crossed
            out_ref[first + p] = (total * inv_scr[pl.ds(first + p, 1), :] + bcol).astype(BF16)
        return 0

    lax.fori_loop(0, 16 // PAIRS, some, 0)


def partner_kernel(left_ref, cross_ref, right_ref, swap_ref, own_ref, give_ref):
    even = lax.rem(lax.axis_index("dap"), 2) == 0
    lane = lax.broadcasted_iota(jnp.int32, (16, 128), 1)

    def channel(c, _):
        near, far = right_ref[c], swap_ref[c]
        lo, hi = jnp.where(even, near, far), jnp.where(even, far, near)
        rows = jnp.concatenate([left_ref[c], cross_ref[c]], axis=0)
        prod = dot_nt(rows, jnp.concatenate([lo, hi, lo, hi], axis=0))
        own_ref[pl.ds(c * 16, 16), :] = jnp.where(lane < 64, prod[0:16], prod[16:32])
        give_ref[c] = jnp.where(lane < 64, prod[32:48], prod[48:64]).astype(BF16)
        return 0

    lax.fori_loop(0, 64, channel, 0, unroll=16)


def triangle_kernel(
    own_ref, right_ref, swap_ref, cross_ref, relay_ref, left_ref, sum_ref, taken_ref, gate_ref, opm_ref,
    fg_ref, fo_ref, wt_ref, tb_ref, out_ref, t_scr,
):
    d, b = lax.axis_index("dap"), lax.axis_index("branch")
    rows = own_ref.shape[0]
    member = member_of_half()
    even = lax.rem(d, 2) == 0
    lane = lax.broadcasted_iota(jnp.int32, (16, 128), 1)

    t_scr[0:1024, :] = jnp.where(
        member, sum_ref[...], taken_ref[...].reshape(1024, 128).astype(F32)
    )

    def channel(c, _):
        near = jnp.where(member, right_ref[c + 64], relay_ref[c])
        far = jnp.where(member, swap_ref[c + 64], cross_ref[c])
        lo, hi = jnp.where(even, near, far), jnp.where(even, far, near)
        prod = dot_nt(left_ref[c + 64], jnp.concatenate([lo, hi, lo, hi], axis=0))
        t_scr[pl.ds((c + 64) * 16, 16), :] = jnp.where(lane < 64, prod[0:16], prod[16:32])
        return 0

    lax.fori_loop(0, 64, channel, 0, unroll=16)

    fg = column(fg_ref[...], 128)
    fo = column(fo_ref[...], 128)
    tb = column(tb_ref[...], 128)
    final = flipped(wt_ref[...]).astype(BF16)

    def finish(p, _):
        x = t_scr[pl.ds(p, 128, stride=16), :]
        mean = jnp.sum(x, axis=0, keepdims=True) * (1.0 / 128)
        delta = x - mean
        spread = jnp.sum(delta * delta, axis=0, keepdims=True) * (1.0 / 128)
        mid = (delta * lax.rsqrt(spread + EPS) * fg + fo).astype(BF16)
        update = (gate_ref[p] * (dot(final, mid) + tb)).astype(BF16)
        total = jnp.transpose(update.astype(F32) + opm_ref[p].astype(F32))
        at = pl.multiple_of(64 * b, 64)
        for h in range(2):
            i = p + h * (rows // 2)
            base = own_ref[i, pl.ds(at, 64), :].astype(F32)
            out_ref[i] = (base + total[64 * h : 64 * h + 64]).astype(BF16)
        return 0

    lax.fori_loop(0, rows // 2, finish, 0, unroll=4)


def call(kernel, shapes, ins, scratch=(), flops=0, size=0, mib=20):
    return pl.pallas_call(
        kernel,
        out_shape=shapes,
        in_specs=ins,
        out_specs=jax.tree.map(lambda _: VMEM, shapes),
        scratch_shapes=list(scratch),
        compiler_params=pltpu.CompilerParams(vmem_limit_bytes=mib * 1024 * 1024),
        cost_estimate=pl.CostEstimate(flops=flops, bytes_accessed=size, transcendentals=0),
    )


SDS = jax.ShapeDtypeStruct


def local(
    homolog_matrix,
    homolog_entry_flags,
    couple_matrix,
    window_amino_flags,
    pairwise_standardize_scaling,
    pairwise_standardize_offset,
    pairwise_factor_matrices,
    pairwise_final_matrix,
    pairwise_final_offset,
    trimul_entry_standardize_scaling,
    trimul_entry_standardize_offset,
    trimul_entry_matrices,
    trimul_entry_offsets,
    trimul_final_standardize_scaling,
    trimul_final_standardize_offset,
    trimul_final_matrix,
    trimul_final_offset,
):
    rows, residues, width = couple_matrix.shape
    seqs = homolog_matrix.shape[0]
    window = window_amino_flags[None, :]
    both = ("branch", "dap")
    block = SDS((128, rows, 128), BF16)
    pair_gain = trimul_entry_standardize_scaling[None]
    pair_bias = trimul_entry_standardize_offset[None]
    offsets = trimul_entry_offsets[None]
    scratch = pltpu.VMEM((rows * 128, 128), F32)
    half = SDS((64, rows, 128), BF16)

    left, right, cross = call(
        sides_kernel,
        [block, block, half],
        [SMEM, HBM, VMEM, VMEM, VMEM, HBM, VMEM],
        [
            pltpu.VMEM(couple_matrix.shape, BF16), pltpu.VMEM((128, 640), BF16),
            scratch, scratch, pltpu.SemaphoreType.DMA((2,)),
        ],
        flops=600_000_000, size=4_000_000, mib=ENTRY_MIB,
    )(
        window_amino_flags, couple_matrix, window, pair_gain, pair_bias, trimul_entry_matrices,
        offsets,
    )
    crossed = lax.ppermute(
        cross, both, [(0, 3), (3, 0), (1, 2), (2, 1), (4, 7), (7, 4), (5, 6), (6, 5)]
    )
    swapped = lax.ppermute(right, both, [(0, 1), (1, 0), (7, 6), (6, 7)])

    homolog, cross = lax.optimization_barrier((homolog_matrix, cross))
    message = call(
        msa_kernel, SDS((4, seqs, 32, 128), BF16), [VMEM] * 6,
        flops=100_000_000, size=2_000_000,
    )(
        homolog, homolog_entry_flags, window,
        pairwise_standardize_scaling[None], pairwise_standardize_offset[None],
        pairwise_factor_matrices.T,
    )
    arrived = lax.all_to_all(message, "dap", 0, 0, tiled=True)

    couple, message = lax.optimization_barrier((couple_matrix, message))
    gate, wcat = call(
        gate_kernel,
        [SDS((rows // 2, 128, 128), F32), SDS((256, 512), BF16)],
        [VMEM] * 6,
        [pltpu.VMEM((1024, 128), F32)],
        flops=200_000_000, size=3_000_000,
    )(couple, pair_gain, pair_bias, trimul_entry_matrices, offsets, pairwise_final_matrix)

    relayed = lax.ppermute(crossed, both, [(3, 2), (2, 3), (4, 5), (5, 4)])
    sums, given = call(
        partner_kernel,
        [SDS((1024, 128), F32), SDS((64, 16, 128), BF16)],
        [VMEM] * 4,
        flops=200_000_000, size=3_000_000,
    )(left, crossed, right, swapped)
    taken = lax.ppermute(given, both, [(0, 3), (1, 2), (7, 4), (6, 5)])

    arrived, given = lax.optimization_barrier((arrived, given))
    opm = call(
        outer_kernel,
        SDS((rows // 2, 128, 128), BF16),
        [VMEM] * 3,
        [
            pltpu.VMEM((2048, 128), F32),
            pltpu.VMEM((1024, 64), F32),
            pltpu.VMEM((64, 2048), BF16),
            pltpu.VMEM((16, 128), F32),
        ],
        flops=1_600_000_000, size=2_000_000,
    )(arrived, wcat, pairwise_final_offset[None])

    return call(
        triangle_kernel,
        SDS((rows, 64, 128), BF16),
        [VMEM] * 14,
        [pltpu.VMEM((128 * 16, 128), F32)],
        flops=400_000_000, size=6_000_000,
    )(
        couple_matrix, right, swapped, crossed, relayed, left, sums, taken, gate, opm,
        trimul_final_standardize_scaling[None], trimul_final_standardize_offset[None],
        trimul_final_matrix, trimul_final_offset[None],
    )


def solution(mesh):
    placed = (
        P(("crop", "dap"), None, None),
        P(("crop", "dap"), None),
        P(("crop", "dap"), None, None),
        P("crop"),
    ) + (P(),) * 13
    return jax.shard_map(
        local,
        mesh=mesh,
        in_specs=placed,
        out_specs=P(("crop", "dap"), "branch", None),
        check_vma=False,
    )
```

time: 107 us -> 62.6 us (0.59)
  the two profiles are of different devices: /device:TPU:690 before, /device:TPU:2 now
where the time goes in v2:
time: 62.6 us; the launch traced here: 62.2 us
  Pallas kernels  25.9 us (41%)
  starting transfers between devices  21.6 us (35%)
  local copies, waits for them, and re-layouts  7.44 us (12%)
  waiting for transfers between devices  6.92 us (11%)
    ppermute x1, starting transfers between devices, local(): swapped = lax.ppermute(right, both, [(0, 1), (1, 0), (7, 6), (6, 7)])  11.5 us
    pallas_call x1, Pallas kernels, local(): call(sides_kernel, [block, block, half], [SMEM, HBM, VMEM, VMEM, VMEM, HB...  9.55 us
    unnamed x54, local copies, waits for them, and re-layouts  6.19 us
    pallas_call x1, Pallas kernels, local(): call(triangle_kernel, SDS((rows, 64, 128), BF16), [VMEM] * 14, [pltpu.VME...  5.36 us
    all_to_all x1, starting transfers between devices, local(): arrived = lax.all_to_all(message, 'dap', 0, 0, tiled=True)  5.35 us
    pallas_call x1, Pallas kernels, local(): call(outer_kernel, SDS((rows // 2, 128, 128), BF16), [VMEM] * 3, [pltpu.V...  5.12 us
    ppermute x1, waiting for transfers between devices, local(): swapped = lax.ppermute(right, both, [(0, 1), (1, 0), (7, 6), (6, 7)])  4.67 us
    pallas_call x1, Pallas kernels, local(): call(partner_kernel, [SDS((1024, 128), F32), SDS((64, 16, 128), BF16)], [...  3.71 us
  transfers between devices with their start and end apart: 5, of which 2 were waited for; matrix products, arithmetic and copies ran while one was open for 0% of the time, Pallas kernels for 18%

profile of v2, /device:TPU:2, one launch (start us, length us, event | category | flops | bytes accessed | tf_op | source)
XLA Modules:
  0.0 62.2 jit_solution(5037154810736072400)
XLA Ops:
  0.0 1.3 %broadcast_in_dim.33.offset.wb_ref = f32[1,640]{1,0:T(1,128)} reshape(f32[640]{0:T(1024)} %param.29) | data formatting | bytes 5120 | tf_op jit(solution)/shard_map/broadcast_in_dim | solution.py:356
  1.3 9.6 %shard_map.163 = (bf16[128,32,128]{2,1,0:T(8,128)(2,1)}, bf16[128,32,128]{2,1,0:T(8,128)(2,1)}, bf16[64,32,128]{2,1,0:T(8,128)(2,1)}) custom-call(s32[128]{0:T(128)} %present.1, bf16[32,128,128]{2,1,0:T(8,128)(2,1)} %own_ref.1, s32[1,128]{1,0:T(1,128)} %bitcast.13, f32[1,128]{1,0:T(1,128)} %bitcast.15, f32[1,128]{1,0:T(1,128)} %bitcast.17, ...), custom_call_target="tpu_custom_call" | custom-call | flops 600000000 | bytes 4000000 | tf_op jit(solution)/shard_map/pallas_call | solution.py:360
  10.8 0.0 copy-start.15
  10.8 11.5 %collective-permute-start = (bf16[128,32,128]{2,1,0:T(8,128)(2,1)}, bf16[128,32,128]{2,1,0:T(8,128)(2,1)S(1)}, u32[]{:S(2)}, u32[]{:S(2)}) collective-permute-start(bf16[128,32,128]{2,1,0:T(8,128)(2,1)} %get-tuple-element.15.right_ref), channel_id=1, source_target_pairs={{0,1},{1,0},{7,6},{6,7},{8,9},{9,8},{15,14},{14,15},{16,17},{17,16... | collective-permute-start | bytes 3145736 | tf_op jit(solution)/shard_map/ppermute | solution.py:376
  22.3 1.9 %collective-permute-start.1 = (bf16[64,32,128]{2,1,0:T(8,128)(2,1)}, bf16[64,32,128]{2,1,0:T(8,128)(2,1)}, u32[]{:S(2)}, u32[]{:S(2)}) collective-permute-start(bf16[64,32,128]{2,1,0:T(8,128)(2,1)} %get-tuple-element.16), channel_id=1, source_target_pairs={{0,3},{3,0},{1,2},{2,1},{4,7},{7,4},{5,6},{6,5},{8,11},{11,8},{9,1... | collective-permute-start | bytes 1572872 | tf_op jit(solution)/shard_map/ppermute | solution.py:373
  24.2 0.0 copy-start.16
  24.2 0.0 copy-done.7
  24.3 0.0 copy-done.13
  24.3 0.0 copy-done.17
  24.3 0.0 copy-done.18
  24.3 0.0 copy-done.15
  24.3 0.6 copy-done.16
  24.9 1.2 %shard_map.165 = bf16[4,16,32,128]{3,2,1,0:T(8,128)(2,1)S(1)} custom-call(bf16[16,128,256]{2,1,0:T(8,128)(2,1)S(1)} %copy-done.7, s32[16,128]{1,0:T(8,128)S(1)} %copy-done.15, s32[1,128]{1,0:T(1,128)S(1)} %bitcast.14, f32[1,256]{1,0:T(1,128)S(1)} %bitcast.11, f32[1,256]{1,0:T(1,128)S(1)} %bitcast.12, bf16[64,256]{1,0:T(8,128)(2,1)S(1)} %bitcast.10), custom_call_target="tpu_custom_call" | custom-call | flops 100000000 | bytes 2000000 | tf_op jit(solution)/shard_map/pallas_call | solution.py:379
  26.1 0.0 copy-start.4
  26.1 0.8 %copy-done.4 = bf16[4,16,32,128]{3,2,1,0:T(8,128)(2,1)} copy-done((bf16[4,16,32,128]{3,2,1,0:T(8,128)(2,1)}, bf16[4,16,32,128]{3,2,1,0:T(8,128)(2,1)S(1)}, u32[]{:S(2)}) %copy-start.4) | copy-done | bytes 524312
  26.9 5.3 %all-to-all-start = ((bf16[4,16,32,128]{3,2,1,0:T(8,128)(2,1)}), bf16[4,16,32,128]{3,2,1,0:T(8,128)(2,1)}, u32[]{:S(2)}, u32[]{:S(2)}) async-start(bf16[4,16,32,128]{3,2,1,0:T(8,128)(2,1)} %copy-done.4), calls=%async_computation | async-start | bytes 1048576 | tf_op jit(solution)/shard_map/all_to_all | solution.py:387
  32.3 2.2 %collective-permute-done.1.cross_ref = bf16[64,32,128]{2,1,0:T(8,128)(2,1)} collective-permute-done((bf16[64,32,128]{2,1,0:T(8,128)(2,1)}, bf16[64,32,128]{2,1,0:T(8,128)(2,1)}, u32[]{:S(2)}, u32[]{:S(2)}) %collective-permute-start.1) | collective-permute-done | bytes 524320 | tf_op jit(solution)/shard_map/ppermute | solution.py:373
  34.5 1.4 %collective-permute-start.2 = (bf16[64,32,128]{2,1,0:T(8,128)(2,1)}, bf16[64,32,128]{2,1,0:T(8,128)(2,1)}, u32[]{:S(2)}, u32[]{:S(2)}) collective-permute-start(bf16[64,32,128]{2,1,0:T(8,128)(2,1)} %collective-permute-done.1.cross_ref), channel_id=1, source_target_pairs={{3,2},{2,3},{4,5},{5,4},{11,10},{10,11},{12,13},{13,12},{19,18},{1... | collective-permute-start | bytes 1572872 | tf_op jit(solution)/shard_map/ppermute | solution.py:398
  36.0 4.7 %collective-permute-done.swap_ref = bf16[128,32,128]{2,1,0:T(8,128)(2,1)S(1)} collective-permute-done((bf16[128,32,128]{2,1,0:T(8,128)(2,1)}, bf16[128,32,128]{2,1,0:T(8,128)(2,1)S(1)}, u32[]{:S(2)}, u32[]{:S(2)}) %collective-permute-start) | collective-permute-done | bytes 1048608 | tf_op jit(solution)/shard_map/ppermute | solution.py:376
  40.6 0.0 copy-done
  40.7 0.0 copy-done.1
  40.7 0.0 copy-start.11
  40.7 3.7 %shard_map.164 = (f32[1024,128]{1,0:T(8,128)S(1)}, bf16[64,16,128]{2,1,0:T(8,128)(2,1)}) custom-call(bf16[128,32,128]{2,1,0:T(8,128)(2,1)S(1)} %copy-done, bf16[64,32,128]{2,1,0:T(8,128)(2,1)} %collective-permute-done.1.cross_ref, bf16[128,32,128]{2,1,0:T(8,128)(2,1)S(1)} %copy-done.1, bf16[128,32,128]{2,1,0:T(8,128)(2,1)S(1)} %collective-permute-done.swap_ref), custom_call_target="tpu_custom_call" | custom-call | flops 200000000 | bytes 3000000 | tf_op jit(solution)/shard_map/pallas_call | solution.py:399
  44.4 0.8 %copy-done.8 = f32[1024,128]{1,0:T(8,128)} copy-done((f32[1024,128]{1,0:T(8,128)}, f32[1024,128]{1,0:T(8,128)S(1)}, u32[]{:S(2)}) %copy-start.8) | copy-done | bytes 524312
  45.2 1.4 %collective-permute-start.3 = (bf16[64,16,128]{2,1,0:T(8,128)(2,1)}, bf16[64,16,128]{2,1,0:T(8,128)(2,1)S(1)}, u32[]{:S(2)}, u32[]{:S(2)}) collective-permute-start(bf16[64,16,128]{2,1,0:T(8,128)(2,1)} %get-tuple-element.19), channel_id=1, source_target_pairs={{0,3},{1,2},{7,4},{6,5},{8,11},{9,10},{15,12},{14,13},{16,19},{17,... | collective-permute-start | bytes 786440 | tf_op jit(solution)/shard_map/ppermute | solution.py:405
  46.6 0.0 copy-done.2
  46.6 0.0 copy-done.10
  46.6 0.0 copy-done.11
  46.7 0.0 copy-done.14
  46.7 0.0 copy-done.19
  46.7 0.0 copy-done.20
  46.7 1.0 %shard_map.166 = (f32[16,128,128]{2,1,0:T(8,128)S(1)}, bf16[256,512]{1,0:T(8,128)(2,1)S(1)}) custom-call(bf16[32,128,128]{2,1,0:T(8,128)(2,1)S(1)} %copy-done.2, f32[1,128]{1,0:T(1,128)S(1)} %bitcast.16, f32[1,128]{1,0:T(1,128)S(1)} %bitcast.18, bf16[128,640]{1,0:T(8,128)(2,1)S(1)} %copy-done.11, f32[1,640]{1,0:T(1,128)S(1)} %copy-done.14, ...), custom_call_target="tpu_custom_call" | custom-call | flops 200000000 | bytes 3000000 | tf_op jit(solution)/shard_map/pallas_call | solution.py:390
  47.7 0.0 copy-start.5
  47.7 1.0 %copy-done.5 = f32[16,128,128]{2,1,0:T(8,128)} copy-done((f32[16,128,128]{2,1,0:T(8,128)}, f32[16,128,128]{2,1,0:T(8,128)S(1)}, u32[]{:S(2)}) %copy-start.5) | copy-done | bytes 1048600
  48.6 0.7 %copy-done.24 = bf16[256,512]{1,0:T(8,128)(2,1)} copy-done((bf16[256,512]{1,0:T(8,128)(2,1)}, bf16[256,512]{1,0:T(8,128)(2,1)S(1)}, u32[]{:S(2)}) %copy-start.24) | copy-done | bytes 262168
  49.4 0.0 all-to-all-done.m_ref
  49.4 0.7 %copy-done.26 = f32[128]{0:T(128)S(1)} copy-done((f32[128]{0:T(128)S(1)}, f32[128]{0:T(128)}, u32[]{:S(2)}) %copy-start.26) | copy-done | bytes 536
  50.0 0.9 %copy-done.25 = bf16[256,512]{1,0:T(8,128)(2,1)S(1)} copy-done((bf16[256,512]{1,0:T(8,128)(2,1)S(1)}, bf16[256,512]{1,0:T(8,128)(2,1)}, u32[]{:S(2)}) %copy-start.25) | copy-done | bytes 262168
  51.0 5.1 %shard_map.167.opm_ref = bf16[16,128,128]{2,1,0:T(8,128)(2,1)S(1)} custom-call(bf16[4,16,32,128]{3,2,1,0:T(8,128)(2,1)} %all-to-all-done.m_ref, bf16[256,512]{1,0:T(8,128)(2,1)S(1)} %copy-done.25, f32[1,128]{1,0:T(1,128)S(1)} %bitcast.22), custom_call_target="tpu_custom_call" | custom-call | flops 1600000000 | bytes 2000000 | tf_op jit(solution)/shard_map/pallas_call | solution.py:408
  56.1 0.0 collective-permute-done.2.relay_ref
  56.1 0.0 collective-permute-done.3.taken_ref
  56.1 0.0 copy-start.21
  56.1 0.0 copy-start.22
  56.1 0.0 copy-start.23
  56.2 0.6 copy-done.21
  56.8 0.0 copy-done.22
  56.8 0.0 copy-done.23
  56.8 5.4 %shard_map.168 = bf16[32,64,128]{2,1,0:T(8,128)(2,1)} custom-call(bf16[32,128,128]{2,1,0:T(8,128)(2,1)S(1)} %copy-done.3, bf16[128,32,128]{2,1,0:T(8,128)(2,1)S(1)} %copy-done.1, bf16[128,32,128]{2,1,0:T(8,128)(2,1)S(1)} %collective-permute-done.swap_ref, bf16[64,32,128]{2,1,0:T(8,128)(2,1)} %collective-permute-done.1.cross_ref, ...), custom_call_target="tpu_custom_call" | custom-call | flops 400000000 | bytes 6000000 | tf_op jit(solution)/shard_map/pallas_call | solution.py:421
  (23 shorter events, 0.0 us)
Async XLA Ops:
  1.3 23.0 %copy-start.7 = (bf16[16,128,256]{2,1,0:T(8,128)(2,1)S(1)}, bf16[16,128,256]{2,1,0:T(8,128)(2,1)}, u32[]{:S(2)}) copy-start(bf16[16,128,256]{2,1,0:T(8,128)(2,1)} %x_ref) | copy-start | bytes 3145732
  1.3 23.0 %copy-start.13 = (bf16[256,64]{0,1:T(8,128)(2,1)S(1)}, bf16[256,64]{0,1:T(8,128)(2,1)}, u32[]{:S(2)}) copy-start(bf16[256,64]{0,1:T(8,128)(2,1)} %param.23) | copy-start | bytes 98308
  1.3 23.0 %copy-start.17 = (f32[256]{0:T(256)S(1)}, f32[256]{0:T(256)}, u32[]{:S(2)}) copy-start(f32[256]{0:T(256)} %param.22) | copy-start | bytes 3076
  1.3 23.0 %copy-start.18 = (s32[128]{0:T(128)S(1)}, s32[128]{0:T(128)}, u32[]{:S(2)}) copy-start(s32[128]{0:T(128)} %present.1) | copy-start | bytes 1540
  10.8 13.5 %copy-start.15 = (s32[16,128]{1,0:T(8,128)S(1)}, s32[16,128]{1,0:T(8,128)}, u32[]{:S(2)}) copy-start(s32[16,128]{1,0:T(8,128)} %flag_ref.1) | copy-start | bytes 24580
  10.8 29.8 %collective-permute-start = (bf16[128,32,128]{2,1,0:T(8,128)(2,1)}, bf16[128,32,128]{2,1,0:T(8,128)(2,1)S(1)}, u32[]{:S(2)}, u32[]{:S(2)}) collective-permute-start(bf16[128,32,128]{2,1,0:T(8,128)(2,1)} %get-tuple-element.15.right_ref), channel_id=1, source_target_pairs={{0,1},{1,0},{7,6},{6,7},{8,9},{9,8},{15,14},{14,15},{16,17},{17,16... | collective-permute-start | bytes 3145736 | tf_op jit(solution)/shard_map/ppermute | solution.py:376
  22.3 12.2 %collective-permute-start.1 = (bf16[64,32,128]{2,1,0:T(8,128)(2,1)}, bf16[64,32,128]{2,1,0:T(8,128)(2,1)}, u32[]{:S(2)}, u32[]{:S(2)}) collective-permute-start(bf16[64,32,128]{2,1,0:T(8,128)(2,1)} %get-tuple-element.16), channel_id=1, source_target_pairs={{0,3},{3,0},{1,2},{2,1},{4,7},{7,4},{5,6},{6,5},{8,11},{11,8},{9,1... | collective-permute-start | bytes 1572872 | tf_op jit(solution)/shard_map/ppermute | solution.py:373
  24.2 0.7 %copy-start.16 = (f32[256]{0:T(256)S(1)}, f32[256]{0:T(256)}, u32[]{:S(2)}) copy-start(f32[256]{0:T(256)} %param.21) | copy-start | bytes 3076
  24.9 15.7 %copy-start = (bf16[128,32,128]{2,1,0:T(8,128)(2,1)S(1)}, bf16[128,32,128]{2,1,0:T(8,128)(2,1)}, u32[]{:S(2)}) copy-start(bf16[128,32,128]{2,1,0:T(8,128)(2,1)} %get-tuple-element.17.left_ref) | copy-start | bytes 3145732
  24.9 15.7 %copy-start.1 = (bf16[128,32,128]{2,1,0:T(8,128)(2,1)S(1)}, bf16[128,32,128]{2,1,0:T(8,128)(2,1)}, u32[]{:S(2)}) copy-start(bf16[128,32,128]{2,1,0:T(8,128)(2,1)} %get-tuple-element.15.right_ref) | copy-start | bytes 3145732
  26.1 0.8 %copy-start.4 = (bf16[4,16,32,128]{3,2,1,0:T(8,128)(2,1)}, bf16[4,16,32,128]{3,2,1,0:T(8,128)(2,1)S(1)}, u32[]{:S(2)}) copy-start(bf16[4,16,32,128]{3,2,1,0:T(8,128)(2,1)S(1)} %shard_map.165) | copy-start | bytes 1572868
  26.9 22.4 %all-to-all-start = ((bf16[4,16,32,128]{3,2,1,0:T(8,128)(2,1)}), bf16[4,16,32,128]{3,2,1,0:T(8,128)(2,1)}, u32[]{:S(2)}, u32[]{:S(2)}) async-start(bf16[4,16,32,128]{3,2,1,0:T(8,128)(2,1)} %copy-done.4), calls=%async_computation | async-start | bytes 1048576 | tf_op jit(solution)/shard_map/all_to_all | solution.py:387
  34.5 21.6 %collective-permute-start.2 = (bf16[64,32,128]{2,1,0:T(8,128)(2,1)}, bf16[64,32,128]{2,1,0:T(8,128)(2,1)}, u32[]{:S(2)}, u32[]{:S(2)}) collective-permute-start(bf16[64,32,128]{2,1,0:T(8,128)(2,1)} %collective-permute-done.1.cross_ref), channel_id=1, source_target_pairs={{3,2},{2,3},{4,5},{5,4},{11,10},{10,11},{12,13},{13,12},{19,18},{1... | collective-permute-start | bytes 1572872 | tf_op jit(solution)/shard_map/ppermute | solution.py:398
  40.7 6.0 %copy-start.2 = (bf16[32,128,128]{2,1,0:T(8,128)(2,1)S(1)}, bf16[32,128,128]{2,1,0:T(8,128)(2,1)}, u32[]{:S(2)}) copy-start(bf16[32,128,128]{2,1,0:T(8,128)(2,1)} %own_ref.1) | copy-start | bytes 3145732
  40.7 6.0 %copy-start.10 = (bf16[1024,128]{1,0:T(8,128)(2,1)S(1)}, bf16[1024,128]{1,0:T(8,128)(2,1)}, u32[]{:S(2)}) copy-start(bf16[1024,128]{1,0:T(8,128)(2,1)} %wf_ref.1) | copy-start | bytes 786436
  40.7 6.0 %copy-start.11 = (bf16[128,640]{1,0:T(8,128)(2,1)S(1)}, bf16[128,640]{1,0:T(8,128)(2,1)}, u32[]{:S(2)}) copy-start(bf16[128,640]{1,0:T(8,128)(2,1)} %w_ref.1) | copy-start | bytes 491524
  40.7 6.0 %copy-start.14 = (f32[1,640]{1,0:T(1,128)S(1)}, f32[1,640]{1,0:T(1,128)}, u32[]{:S(2)}) copy-start(f32[1,640]{1,0:T(1,128)} %broadcast_in_dim.33.offset.wb_ref) | copy-start | bytes 7684
  44.4 0.8 %copy-start.8 = (f32[1024,128]{1,0:T(8,128)}, f32[1024,128]{1,0:T(8,128)S(1)}, u32[]{:S(2)}) copy-start(f32[1024,128]{1,0:T(8,128)S(1)} %get-tuple-element.18.sum_ref) | copy-start | bytes 1572868
  45.2 1.5 %copy-start.19 = (f32[128]{0:T(128)S(1)}, f32[128]{0:T(128)}, u32[]{:S(2)}) copy-start(f32[128]{0:T(128)} %param.26) | copy-start | bytes 1540
  45.2 1.5 %copy-start.20 = (f32[128]{0:T(128)S(1)}, f32[128]{0:T(128)}, u32[]{:S(2)}) copy-start(f32[128]{0:T(128)} %param.27) | copy-start | bytes 1540
  45.2 10.9 %collective-permute-start.3 = (bf16[64,16,128]{2,1,0:T(8,128)(2,1)}, bf16[64,16,128]{2,1,0:T(8,128)(2,1)S(1)}, u32[]{:S(2)}, u32[]{:S(2)}) collective-permute-start(bf16[64,16,128]{2,1,0:T(8,128)(2,1)} %get-tuple-element.19), channel_id=1, source_target_pairs={{0,3},{1,2},{7,4},{6,5},{8,11},{9,10},{15,12},{14,13},{16,19},{17,... | collective-permute-start | bytes 786440 | tf_op jit(solution)/shard_map/ppermute | solution.py:405
  47.7 1.0 %copy-start.5 = (f32[16,128,128]{2,1,0:T(8,128)}, f32[16,128,128]{2,1,0:T(8,128)S(1)}, u32[]{:S(2)}) copy-start(f32[16,128,128]{2,1,0:T(8,128)S(1)} %get-tuple-element.22.gate_ref) | copy-start | bytes 3145732
  48.6 0.7 %copy-start.24 = (bf16[256,512]{1,0:T(8,128)(2,1)}, bf16[256,512]{1,0:T(8,128)(2,1)S(1)}, u32[]{:S(2)}) copy-start(bf16[256,512]{1,0:T(8,128)(2,1)S(1)} %get-tuple-element.24.wcat_ref) | copy-start | bytes 786436
  49.4 0.7 %copy-start.26 = (f32[128]{0:T(128)S(1)}, f32[128]{0:T(128)}, u32[]{:S(2)}) copy-start(f32[128]{0:T(128)} %param.25) | copy-start | bytes 1540
  50.0 0.9 %copy-start.25 = (bf16[256,512]{1,0:T(8,128)(2,1)S(1)}, bf16[256,512]{1,0:T(8,128)(2,1)}, u32[]{:S(2)}) copy-start(bf16[256,512]{1,0:T(8,128)(2,1)} %copy-done.24) | copy-start | bytes 786436
  51.0 5.2 %copy-start.3 = (bf16[32,128,128]{2,1,0:T(8,128)(2,1)S(1)}, bf16[32,128,128]{2,1,0:T(8,128)(2,1)}, u32[]{:S(2)}) copy-start(bf16[32,128,128]{2,1,0:T(8,128)(2,1)} %own_ref.1) | copy-start | bytes 3145732
  51.0 5.2 %copy-start.6 = (f32[16,128,128]{2,1,0:T(8,128)S(1)}, f32[16,128,128]{2,1,0:T(8,128)}, u32[]{:S(2)}) copy-start(f32[16,128,128]{2,1,0:T(8,128)} %copy-done.5) | copy-start | bytes 3145732
  51.0 5.2 %copy-start.9 = (f32[1024,128]{1,0:T(8,128)S(1)}, f32[1024,128]{1,0:T(8,128)}, u32[]{:S(2)}) copy-start(f32[1024,128]{1,0:T(8,128)} %copy-done.8) | copy-start | bytes 1572868
  51.0 5.2 %copy-start.12 = (bf16[128,128]{1,0:T(8,128)(2,1)S(1)}, bf16[128,128]{1,0:T(8,128)(2,1)}, u32[]{:S(2)}) copy-start(bf16[128,128]{1,0:T(8,128)(2,1)} %wt_ref.1) | copy-start | bytes 98308
  56.1 0.7 %copy-start.21 = (f32[128]{0:T(128)S(1)}, f32[128]{0:T(128)}, u32[]{:S(2)}) copy-start(f32[128]{0:T(128)} %param.30) | copy-start | bytes 1540
  56.1 0.7 %copy-start.22 = (f32[128]{0:T(128)S(1)}, f32[128]{0:T(128)}, u32[]{:S(2)}) copy-start(f32[128]{0:T(128)} %param.31) | copy-start | bytes 1540
  56.1 0.7 %copy-start.23 = (f32[128]{0:T(128)S(1)}, f32[128]{0:T(128)}, u32[]{:S(2)}) copy-start(f32[128]{0:T(128)} %param.33) | copy-start | bytes 1540

commit v3 on v2

--- a/solution.py
+++ b/solution.py
@@ -13,8 +13,11 @@
 SMEM = pl.BlockSpec(memory_space=pltpu.SMEM)
 HBM = pl.BlockSpec(memory_space=pltpu.HBM)
 ENTRY_MIB = 56
-BLOCK = 16
-PAIRS = 4
+BLOCK = 32
+SIDE_PITCH = 132
+SUM_PITCH = 24
+MSA_PITCH = 40
+PAIRS = 16
 
 
 def dot(a, b):
@@ -65,7 +68,8 @@
 def gate_weights(w_ref, wb_ref, bias, at):
     wt = flipped(w_ref[:, at : at + 256])
     shift = jnp.sum(wt * bias, axis=1, keepdims=True)
-    col = column(wb_ref[:, at : at + 256], 128) + shift
+    rows = [wb_ref[k : k + 1, :] for k in (at // 128, at // 128 + 1)]
+    col = column(jnp.concatenate(rows, axis=1), 128) + shift
     half = jnp.where(lax.broadcasted_iota(jnp.int32, (256, 128), 0) < 128, 0.5, 1.0)
     col = col * half
     return (wt * half).astype(BF16), jnp.concatenate([col, col], axis=1)
@@ -89,14 +93,13 @@
             for wt, col, scr in sides:
                 result = gated(wt, col, gained[lanes], scale[:, lanes], live)
                 for h in range(2):
-                    scr[pl.ds((i + v + h) * 128, 128), :] = result[:, 128 * h : 128 * h + 128]
+                    scr[pl.ds((i + v + h) * SIDE_PITCH, 128), :] = result[:, 128 * h : 128 * h + 128]
         return 0
 
     lax.fori_loop(0, rows // BLOCK, some, 0)
 
 
-def msa_kernel(x_ref, flag_ref, window_ref, gain_ref, bias_ref, wt_ref, out_ref):
-    b = lax.axis_index("branch")
+def message_part(b, x_ref, flag_ref, window_ref, gain_ref, bias_ref, wt_ref, out_ref):
     seqs, residues, width = x_ref.shape
     ones = jnp.full((8, width), 1.0 / width, BF16)
     centre = centring(width, 1)
@@ -140,24 +143,31 @@
 
 def sides_kernel(
     present, couple, window_ref, gain_ref, bias_ref, weight, offset,
-    left_ref, right_ref, cross_ref, couple_v, weight_v, left_scr, right_scr, sems,
+    left_ref, lower_ref, upper_ref, cross_ref, offset_out,
+    couple_v, weight_v, offset_v, left_scr, right_scr, sems,
 ):
     rows = couple_v.shape[0]
     member = member_of_half()
     copies = [
         pltpu.make_async_copy(src, dst, sems.at[k])
-        for k, (src, dst) in enumerate([(weight, weight_v), (couple, couple_v)])
+        for k, (src, dst) in enumerate(
+            [(weight, weight_v)]
+            + [(offset.at[pl.ds(128 * t, 128)], offset_v.at[t]) for t in range(5)]
+            + [(couple, couple_v)]
+        )
     ]
     for copy in copies:
         copy.start()
-    copies[0].wait()
+    for copy in copies[:-1]:
+        copy.wait()
+    offset_out[...] = offset_v[...]
     ones = jnp.full((8, 128), 1.0 / 128, BF16)
     bias = bias_ref[...]
     sides = [
-        (*gate_weights(weight_v, offset, bias, 256 * k), scr)
+        (*gate_weights(weight_v, offset_v, bias, 256 * k), scr)
         for k, scr in enumerate((left_scr, right_scr))
     ]
-    copies[1].wait()
+    copies[-1].wait()
     live_k = window_ref[...].astype(F32)
     project_rows(
         couple_v, present, lax.axis_index("dap") * rows, rows, live_k,
@@ -165,26 +175,28 @@
     )
 
     def turn(c, _):
-        left = [left_scr[pl.ds(c + 64 * h, rows, stride=128), :].astype(BF16) for h in range(2)]
-        right = [right_scr[pl.ds(c + 64 * h, rows, stride=128), :].astype(BF16) for h in range(2)]
+        left = [left_scr[pl.ds(c + 64 * h, rows, stride=SIDE_PITCH), :].astype(BF16) for h in range(2)]
+        right = [right_scr[pl.ds(c + 64 * h, rows, stride=SIDE_PITCH), :].astype(BF16) for h in range(2)]
         for h in range(2):
             left_ref[c + 64 * h] = left[h]
-            right_ref[c + 64 * h] = right[h]
+        lower_ref[c], upper_ref[c] = right
         cross_ref[c] = jnp.where(member, right[1], left[0])
         return 0
 
     lax.fori_loop(0, 64, turn, 0, unroll=8)
 
 
-def gate_kernel(
-    x_ref, gain_ref, bias_ref, w_ref, wb_ref, wf_ref, gate_ref, wcat_ref, wf_scr,
+def middle_kernel(
+    homolog, flag, window, m_gain, m_bias, m_weight,
+    x_ref, gain_ref, bias_ref, w_ref, wb_ref, wf_ref, message_ref, gate_ref, wcat_ref, wf_scr,
 ):
     b = lax.axis_index("branch")
+    message_part(b, homolog, flag, window, m_gain, m_bias, m_weight, message_ref)
     rows = x_ref.shape[0]
     ones = jnp.full((8, 128), 1.0 / 128, BF16)
     centre, gain = centring(128, 2), gain_ref[...]
     wg = flipped(w_ref[:, 512:640])
-    gcol = column(wb_ref[:, 512:640], 128) + jnp.sum(wg * bias_ref[...], axis=1, keepdims=True)
+    gcol = column(wb_ref[4:5, :], 128) + jnp.sum(wg * bias_ref[...], axis=1, keepdims=True)
     wg, gcol = (0.5 * wg).astype(BF16), 0.5 * gcol
     at = pl.multiple_of(64 * b, 64)
 
@@ -198,19 +210,21 @@
         part = projected[:, 128 * p : 128 * p + 128] + gcol
         gate_ref[p] = 0.5 * jnp.tanh(part) + 0.5
 
-    wf_scr[...] = wf_ref[...].astype(F32)
+    for c in range(32):
+        wf_scr[pl.ds(c * MSA_PITCH, 32), :] = wf_ref[pl.ds(c * 32, 32), :].astype(F32)
     for p in range(2):
         for t in range(4):
-            parts = [wf_scr[pl.ds(p * 16 + 4 * t + u, 32, stride=32), :] for u in range(4)]
+            parts = [wf_scr[pl.ds(p * 16 + 4 * t + u, 32, stride=MSA_PITCH), :] for u in range(4)]
             block = jnp.transpose(jnp.concatenate(parts, axis=0))
             wcat_ref[128 * p : 128 * p + 128, 128 * t : 128 * t + 128] = block.astype(BF16)
 
 
 def outer_kernel(m_ref, wcat_ref, fb_ref, out_ref, m_scr, a_scr, r_scr, inv_scr):
-    m_scr[...] = m_ref[...].reshape(2048, 128).astype(F32)
+    for k in range(64):
+        m_scr[pl.ds(k * MSA_PITCH, 32), :] = m_ref[k // 16, k % 16].astype(F32)
 
     def row(k):
-        return m_scr[pl.ds(k, 64, stride=32), :]
+        return m_scr[pl.ds(k, 64, stride=MSA_PITCH), :]
 
     flags = row(24)
     count = dot(jnp.transpose(flags).astype(BF16), flags.astype(BF16))[0:32]
@@ -222,7 +236,7 @@
     for r in range(8):
         turned = jnp.transpose(row(r))
         for q in range(4):
-            a_scr[pl.ds((q * 8 + r) * 32, 32), :] = turned[32 * q : 32 * q + 32]
+            a_scr[pl.ds((q * 8 + r) * MSA_PITCH, 32), :] = turned[32 * q : 32 * q + 32]
     for t in range(16):
         r_scr[:, 128 * t : 128 * t + 128] = row(8 + t).astype(BF16)
 
@@ -232,7 +246,7 @@
 
     def some(u, _):
         first = PAIRS * u
-        a = [a_scr[pl.ds(first + p + 16 * h, 32, stride=32), :] for p in range(PAIRS) for h in range(2)]
+        a = [a_scr[pl.ds(first + p + 16 * h, 32, stride=MSA_PITCH), :] for p in range(PAIRS) for h in range(2)]
         products = dot(jnp.concatenate(a, axis=0).astype(BF16), r_scr[...]).astype(BF16)
         for p in range(PAIRS):
             lo, hi = products[64 * p : 64 * p + 32], products[64 * p + 32 : 64 * p + 64]
@@ -251,18 +265,17 @@
 
 def partner_kernel(left_ref, cross_ref, right_ref, swap_ref, own_ref, give_ref):
     even = lax.rem(lax.axis_index("dap"), 2) == 0
-    lane = lax.broadcasted_iota(jnp.int32, (16, 128), 1)
 
     def channel(c, _):
         near, far = right_ref[c], swap_ref[c]
         lo, hi = jnp.where(even, near, far), jnp.where(even, far, near)
         rows = jnp.concatenate([left_ref[c], cross_ref[c]], axis=0)
-        prod = dot_nt(rows, jnp.concatenate([lo, hi, lo, hi], axis=0))
-        own_ref[pl.ds(c * 16, 16), :] = jnp.where(lane < 64, prod[0:16], prod[16:32])
-        give_ref[c] = jnp.where(lane < 64, prod[32:48], prod[48:64]).astype(BF16)
-        return 0
-
-    lax.fori_loop(0, 64, channel, 0, unroll=16)
+        prod = dot_nt(rows, jnp.concatenate([lo, hi], axis=0))
+        own_ref[pl.ds(c * 16, 16), :] = jnp.concatenate([prod[0:16], prod[16:32]], axis=1)
+        give_ref[c] = jnp.concatenate([prod[32:48], prod[48:64]], axis=1).astype(BF16)
+        return 0
+
+    lax.fori_loop(0, 64, channel, 0, unroll=32)
 
 
 def triangle_kernel(
@@ -273,21 +286,22 @@
     rows = own_ref.shape[0]
     member = member_of_half()
     even = lax.rem(d, 2) == 0
-    lane = lax.broadcasted_iota(jnp.int32, (16, 128), 1)
-
-    t_scr[0:1024, :] = jnp.where(
-        member, sum_ref[...], taken_ref[...].reshape(1024, 128).astype(F32)
-    )
+
+    for c in range(64):
+        t_scr[pl.ds(c * SUM_PITCH, 16), :] = jnp.where(
+            member, sum_ref[pl.ds(c * 16, 16), :], taken_ref[c].astype(F32)
+        )
 
     def channel(c, _):
-        near = jnp.where(member, right_ref[c + 64], relay_ref[c])
-        far = jnp.where(member, swap_ref[c + 64], cross_ref[c])
+        near = jnp.where(member, right_ref[c], relay_ref[c])
+        far = jnp.where(member, swap_ref[c], cross_ref[c])
         lo, hi = jnp.where(even, near, far), jnp.where(even, far, near)
-        prod = dot_nt(left_ref[c + 64], jnp.concatenate([lo, hi, lo, hi], axis=0))
-        t_scr[pl.ds((c + 64) * 16, 16), :] = jnp.where(lane < 64, prod[0:16], prod[16:32])
-        return 0
-
-    lax.fori_loop(0, 64, channel, 0, unroll=16)
+        prod = dot_nt(left_ref[c + 64], jnp.concatenate([lo, hi], axis=0))
+        sums = jnp.concatenate([prod[0:16], prod[16:32]], axis=1)
+        t_scr[pl.ds((c + 64) * SUM_PITCH, 16), :] = sums
+        return 0
+
+    lax.fori_loop(0, 64, channel, 0, unroll=32)
 
     fg = column(fg_ref[...], 128)
     fo = column(fo_ref[...], 128)
@@ -295,7 +309,7 @@
     final = flipped(wt_ref[...]).astype(BF16)
 
     def finish(p, _):
-        x = t_scr[pl.ds(p, 128, stride=16), :]
+        x = t_scr[pl.ds(p, 128, stride=SUM_PITCH), :]
         mean = jnp.sum(x, axis=0, keepdims=True) * (1.0 / 128)
         delta = x - mean
         spread = jnp.sum(delta * delta, axis=0, keepdims=True) * (1.0 / 128)
@@ -309,7 +323,7 @@
             out_ref[i] = (base + total[64 * h : 64 * h + 64]).astype(BF16)
         return 0
 
-    lax.fori_loop(0, rows // 2, finish, 0, unroll=4)
+    lax.fori_loop(0, rows // 2, finish, 0, unroll=16)
 
 
 def call(kernel, shapes, ins, scratch=(), flops=0, size=0, mib=20):
@@ -353,55 +367,52 @@
     block = SDS((128, rows, 128), BF16)
     pair_gain = trimul_entry_standardize_scaling[None]
     pair_bias = trimul_entry_standardize_offset[None]
-    offsets = trimul_entry_offsets[None]
-    scratch = pltpu.VMEM((rows * 128, 128), F32)
+    scratch = pltpu.VMEM((rows * SIDE_PITCH, 128), F32)
     half = SDS((64, rows, 128), BF16)
 
-    left, right, cross = call(
+    left, lower, upper, cross, offsets = call(
         sides_kernel,
-        [block, block, half],
-        [SMEM, HBM, VMEM, VMEM, VMEM, HBM, VMEM],
+        [block, half, half, half, SDS((8, 128), F32)],
+        [SMEM, HBM, VMEM, VMEM, VMEM, HBM, HBM],
         [
             pltpu.VMEM(couple_matrix.shape, BF16), pltpu.VMEM((128, 640), BF16),
-            scratch, scratch, pltpu.SemaphoreType.DMA((2,)),
+            pltpu.VMEM((8, 128), F32), scratch, scratch, pltpu.SemaphoreType.DMA((7,)),
         ],
         flops=600_000_000, size=4_000_000, mib=ENTRY_MIB,
     )(
         window_amino_flags, couple_matrix, window, pair_gain, pair_bias, trimul_entry_matrices,
-        offsets,
-    )
+        trimul_entry_offsets,
+    )
+    swap = [(0, 1), (1, 0), (7, 6), (6, 7)]
     crossed = lax.ppermute(
         cross, both, [(0, 3), (3, 0), (1, 2), (2, 1), (4, 7), (7, 4), (5, 6), (6, 5)]
     )
-    swapped = lax.ppermute(right, both, [(0, 1), (1, 0), (7, 6), (6, 7)])
+    swapped = lax.ppermute(lower, both, swap)
 
     homolog, cross = lax.optimization_barrier((homolog_matrix, cross))
-    message = call(
-        msa_kernel, SDS((4, seqs, 32, 128), BF16), [VMEM] * 6,
-        flops=100_000_000, size=2_000_000,
+    message, gate, wcat = call(
+        middle_kernel,
+        [SDS((4, seqs, 32, 128), BF16), SDS((rows // 2, 128, 128), F32), SDS((256, 512), BF16)],
+        [VMEM] * 12,
+        [pltpu.VMEM((32 * MSA_PITCH, 128), F32)],
+        flops=300_000_000, size=5_000_000, mib=ENTRY_MIB,
     )(
         homolog, homolog_entry_flags, window,
         pairwise_standardize_scaling[None], pairwise_standardize_offset[None],
         pairwise_factor_matrices.T,
+        couple_matrix, pair_gain, pair_bias, trimul_entry_matrices, offsets, pairwise_final_matrix,
     )
     arrived = lax.all_to_all(message, "dap", 0, 0, tiled=True)
 
-    couple, message = lax.optimization_barrier((couple_matrix, message))
-    gate, wcat = call(
-        gate_kernel,
-        [SDS((rows // 2, 128, 128), F32), SDS((256, 512), BF16)],
-        [VMEM] * 6,
-        [pltpu.VMEM((1024, 128), F32)],
-        flops=200_000_000, size=3_000_000,
-    )(couple, pair_gain, pair_bias, trimul_entry_matrices, offsets, pairwise_final_matrix)
-
+    crossed, swapped, upper = lax.optimization_barrier((crossed, swapped, upper))
     relayed = lax.ppermute(crossed, both, [(3, 2), (2, 3), (4, 5), (5, 4)])
+    swapped_upper = lax.ppermute(upper, both, swap)
     sums, given = call(
         partner_kernel,
         [SDS((1024, 128), F32), SDS((64, 16, 128), BF16)],
         [VMEM] * 4,
         flops=200_000_000, size=3_000_000,
-    )(left, crossed, right, swapped)
+    )(left, crossed, lower, swapped)
     taken = lax.ppermute(given, both, [(0, 3), (1, 2), (7, 4), (6, 5)])
 
     arrived, given = lax.optimization_barrier((arrived, given))
@@ -410,8 +421,8 @@
         SDS((rows // 2, 128, 128), BF16),
         [VMEM] * 3,
         [
-            pltpu.VMEM((2048, 128), F32),
-            pltpu.VMEM((1024, 64), F32),
+            pltpu.VMEM((64 * MSA_PITCH, 128), F32),
+            pltpu.VMEM((32 * MSA_PITCH, 64), F32),
             pltpu.VMEM((64, 2048), BF16),
             pltpu.VMEM((16, 128), F32),
         ],
@@ -422,10 +433,10 @@
         triangle_kernel,
         SDS((rows, 64, 128), BF16),
         [VMEM] * 14,
-        [pltpu.VMEM((128 * 16, 128), F32)],
+        [pltpu.VMEM((128 * SUM_PITCH, 128), F32)],
         flops=400_000_000, size=6_000_000,
     )(
-        couple_matrix, right, swapped, crossed, relayed, left, sums, taken, gate, opm,
+        couple_matrix, upper, swapped_upper, crossed, relayed, left, sums, taken, gate, opm,
         trimul_final_standardize_scaling[None], trimul_final_standardize_offset[None],
         trimul_final_matrix, trimul_final_offset[None],
     )

time: 62.6 us -> 51.2 us (0.82)
  the two profiles are of different devices: /device:TPU:2 before, /device:TPU:6 now
where the time goes in v3:
time: 51.2 us; the launch traced here: 50.2 us
  starting transfers between devices  22.4 us (44%)
  Pallas kernels  19 us (37%)
  waiting for transfers between devices  6.59 us (13%)
  local copies, waits for them, and re-layouts  2.1 us (4%)
    ppermute x1, starting transfers between devices, local(): lax.ppermute(cross, both, [(0, 3), (3, 0), (1, 2), (2, 1), (4, 7), (7, 4)...  11.4 us
    pallas_call x1, Pallas kernels, local(): call(sides_kernel, [block, half, half, half, SDS((8, 128), F32)], [SMEM,...  6.16 us
    all_to_all x1, starting transfers between devices, local(): arrived = lax.all_to_all(message, 'dap', 0, 0, tiled=True)  4.81 us
    pallas_call x1, Pallas kernels, local(): call(middle_kernel, [SDS((4, seqs, 32, 128), BF16), SDS((rows // 2, 128,...  4.58 us
    pallas_call x1, Pallas kernels, local(): call(triangle_kernel, SDS((rows, 64, 128), BF16), [VMEM] * 14, [pltpu.VME...  3.83 us
    all_to_all x1, waiting for transfers between devices, local(): arrived = lax.all_to_all(message, 'dap', 0, 0, tiled=True)  3.42 us
    ppermute x1, waiting for transfers between devices, local(): taken = lax.ppermute(given, both, [(0, 3), (1, 2), (7, 4), (6, 5)])  3.16 us
    pallas_call x1, Pallas kernels, local(): call(outer_kernel, SDS((rows // 2, 128, 128), BF16), [VMEM] * 3, [pltpu.V...  2.78 us
  transfers between devices with their start and end apart: 6, of which 2 were waited for; matrix products, arithmetic and copies ran while one was open for 0% of the time, Pallas kernels for 18%

profile of v3, /device:TPU:6, one launch (start us, length us, event | category | flops | bytes accessed | tf_op | source)
XLA Modules:
  0.0 50.2 jit_solution(6218688157367418817)
XLA Ops:
  0.0 6.2 %shard_map.163 = (bf16[128,32,128]{2,1,0:T(8,128)(2,1)}, bf16[64,32,128]{2,1,0:T(8,128)(2,1)}, bf16[64,32,128]{2,1,0:T(8,128)(2,1)}, bf16[64,32,128]{2,1,0:T(8,128)(2,1)}, f32[8,128]{1,0:T(8,128)}) custom-call(s32[128]{0:T(128)} %present.1, bf16[32,128,128]{2,1,0:T(8,128)(2,1)} %own_ref.1, s32[1,128]{1,0:T(1,128)} %bitcast.17, f32[1,128]{1,0:T(1,128)} %bitcast.19, ...), custom_call_target="tpu_custom_call" | custom-call | flops 600000000 | bytes 4000000 | tf_op jit(solution)/shard_map/pallas_call | solution.py:373
  6.2 11.4 %collective-permute-start = (bf16[64,32,128]{2,1,0:T(8,128)(2,1)}, bf16[64,32,128]{2,1,0:T(8,128)(2,1)S(1)}, u32[]{:S(2)}, u32[]{:S(2)}) collective-permute-start(bf16[64,32,128]{2,1,0:T(8,128)(2,1)} %get-tuple-element.20), channel_id=1, source_target_pairs={{0,3},{3,0},{1,2},{2,1},{4,7},{7,4},{5,6},{6,5},{8,11},{11,8},{9,1... | collective-permute-start | bytes 1572872 | tf_op jit(solution)/shard_map/ppermute | solution.py:387
  17.6 0.7 %collective-permute-start.1 = (bf16[64,32,128]{2,1,0:T(8,128)(2,1)}, bf16[64,32,128]{2,1,0:T(8,128)(2,1)S(1)}, u32[]{:S(2)}, u32[]{:S(2)}) collective-permute-start(bf16[64,32,128]{2,1,0:T(8,128)(2,1)} %get-tuple-element.21.right_ref), channel_id=1, source_target_pairs={{0,1},{1,0},{7,6},{6,7},{8,9},{9,8},{15,14},{14,15},{16,17},{17,16... | collective-permute-start | bytes 1572872 | tf_op jit(solution)/shard_map/ppermute | solution.py:390
  18.3 0.0 copy-start.3
  18.3 4.6 %shard_map.165 = (bf16[4,16,32,128]{3,2,1,0:T(8,128)(2,1)}, f32[16,128,128]{2,1,0:T(8,128)}, bf16[256,512]{1,0:T(8,128)(2,1)}) custom-call(bf16[16,128,256]{2,1,0:T(8,128)(2,1)} %homolog, s32[16,128]{1,0:T(8,128)} %flag.1, s32[1,128]{1,0:T(1,128)} %bitcast.18, f32[1,256]{1,0:T(1,128)} %bitcast.15, f32[1,256]{1,0:T(1,128)} %bitcast.16, ...), custom_call_target="tpu_custom_call" | custom-call | flops 300000000 | bytes 5000000 | tf_op jit(solution)/shard_map/pallas_call | solution.py:393
  22.9 0.0 copy-start.1
  22.9 4.8 %all-to-all-start = ((bf16[4,16,32,128]{3,2,1,0:T(8,128)(2,1)}), bf16[4,16,32,128]{3,2,1,0:T(8,128)(2,1)S(1)}, u32[]{:S(2)}, u32[]{:S(2)}) async-start(bf16[4,16,32,128]{3,2,1,0:T(8,128)(2,1)} %get-tuple-element.32), calls=%async_computation | async-start | bytes 1048576 | tf_op jit(solution)/shard_map/all_to_all | solution.py:405
  27.7 0.0 collective-permute-done.cross_ref
  27.7 0.0 collective-permute-done.1.swap_ref
  27.7 2.8 %collective-permute-start.3 = (bf16[64,32,128]{2,1,0:T(8,128)(2,1)S(1)}, bf16[64,32,128]{2,1,0:T(8,128)(2,1)}, u32[]{:S(2)}, u32[]{:S(2)}) collective-permute-start(bf16[64,32,128]{2,1,0:T(8,128)(2,1)S(1)} %collective-permute-done.cross_ref), channel_id=1, source_target_pairs={{3,2},{2,3},{4,5},{5,4},{11,10},{10,11},{12,13},{13,12},{19,18},{1... | collective-permute-start | bytes 1572872 | tf_op jit(solution)/shard_map/ppermute | solution.py:408
  30.5 1.5 %collective-permute-start.2 = (bf16[64,32,128]{2,1,0:T(8,128)(2,1)}, bf16[64,32,128]{2,1,0:T(8,128)(2,1)}, u32[]{:S(2)}, u32[]{:S(2)}) collective-permute-start(bf16[64,32,128]{2,1,0:T(8,128)(2,1)} %get-tuple-element.23.right_ref), channel_id=1, source_target_pairs={{0,1},{1,0},{7,6},{6,7},{8,9},{9,8},{15,14},{14,15},{16,17},{17,16... | collective-permute-start | bytes 1572872 | tf_op jit(solution)/shard_map/ppermute | solution.py:409
  31.9 0.0 copy-done.3
  31.9 0.0 copy-done.1
  31.9 0.0 copy-start.11
  31.9 1.7 %shard_map.164 = (f32[1024,128]{1,0:T(8,128)S(1)}, bf16[64,16,128]{2,1,0:T(8,128)(2,1)}) custom-call(bf16[128,32,128]{2,1,0:T(8,128)(2,1)S(1)} %copy-done.1, bf16[64,32,128]{2,1,0:T(8,128)(2,1)S(1)} %collective-permute-done.cross_ref, bf16[64,32,128]{2,1,0:T(8,128)(2,1)S(1)} %copy-done.3, bf16[64,32,128]{2,1,0:T(8,128)(2,1)S(1)} %collective-permute-done.1.swap_ref), custom_call_target="tpu_custom_call" | custom-call | flops 200000000 | bytes 3000000 | tf_op jit(solution)/shard_map/pallas_call | solution.py:410
  33.6 0.0 copy-start.5
  33.6 0.8 %copy-done.5 = f32[1024,128]{1,0:T(8,128)} copy-done((f32[1024,128]{1,0:T(8,128)}, f32[1024,128]{1,0:T(8,128)S(1)}, u32[]{:S(2)}) %copy-start.5) | copy-done | bytes 524312
  34.4 1.3 %collective-permute-start.4 = (bf16[64,16,128]{2,1,0:T(8,128)(2,1)}, bf16[64,16,128]{2,1,0:T(8,128)(2,1)S(1)}, u32[]{:S(2)}, u32[]{:S(2)}) collective-permute-start(bf16[64,16,128]{2,1,0:T(8,128)(2,1)} %get-tuple-element.28), channel_id=1, source_target_pairs={{0,3},{1,2},{7,4},{6,5},{8,11},{9,10},{15,12},{14,13},{16,19},{17,... | collective-permute-start | bytes 786440 | tf_op jit(solution)/shard_map/ppermute | solution.py:416
  35.7 3.4 %all-to-all-done.m_ref = bf16[4,16,32,128]{3,2,1,0:T(8,128)(2,1)S(1)} async-done(((bf16[4,16,32,128]{3,2,1,0:T(8,128)(2,1)}), bf16[4,16,32,128]{3,2,1,0:T(8,128)(2,1)S(1)}, u32[]{:S(2)}, u32[]{:S(2)}) %all-to-all-start) | async-done | bytes 524320 | tf_op jit(solution)/shard_map/all_to_all | solution.py:405
  39.1 0.0 copy-start.12
  39.1 0.0 copy-done.11
  39.1 0.7 %copy-done.12 = f32[128]{0:T(128)S(1)} copy-done((f32[128]{0:T(128)S(1)}, f32[128]{0:T(128)}, u32[]{:S(2)}) %copy-start.12) | copy-done | bytes 536
  39.7 0.0 copy-start
  39.7 0.0 copy-start.2
  39.7 0.0 copy-start.4
  39.7 0.0 copy-start.6
  39.8 0.0 copy-start.7
  39.8 2.8 %shard_map.166.opm_ref = bf16[16,128,128]{2,1,0:T(8,128)(2,1)S(1)} custom-call(bf16[4,16,32,128]{3,2,1,0:T(8,128)(2,1)S(1)} %all-to-all-done.m_ref, bf16[256,512]{1,0:T(8,128)(2,1)S(1)} %copy-done.11, f32[1,128]{1,0:T(1,128)S(1)} %bitcast.13), custom_call_target="tpu_custom_call" | custom-call | flops 1600000000 | bytes 2000000 | tf_op jit(solution)/shard_map/pallas_call | solution.py:419
  42.6 3.2 %collective-permute-done.4.taken_ref = bf16[64,16,128]{2,1,0:T(8,128)(2,1)S(1)} collective-permute-done((bf16[64,16,128]{2,1,0:T(8,128)(2,1)}, bf16[64,16,128]{2,1,0:T(8,128)(2,1)S(1)}, u32[]{:S(2)}, u32[]{:S(2)}) %collective-permute-start.4) | collective-permute-done | bytes 262176 | tf_op jit(solution)/shard_map/ppermute | solution.py:416
  45.7 0.0 collective-permute-done.3.relay_ref
  45.7 0.0 collective-permute-done.2.swap_ref
  45.7 0.0 copy-start.8
  45.7 0.0 copy-start.9
  45.7 0.0 copy-start.10
  45.7 0.0 copy-done
  45.8 0.0 copy-done.2
  45.8 0.0 copy-done.4
  45.8 0.0 copy-done.6
  45.8 0.0 copy-done.7
  45.8 0.6 %copy-done.8 = f32[128]{0:T(128)S(1)} copy-done((f32[128]{0:T(128)S(1)}, f32[128]{0:T(128)}, u32[]{:S(2)}) %copy-start.8) | copy-done | bytes 536
  46.4 0.0 copy-done.9
  46.4 0.0 copy-done.10
  46.4 3.8 %shard_map.167 = bf16[32,64,128]{2,1,0:T(8,128)(2,1)} custom-call(bf16[32,128,128]{2,1,0:T(8,128)(2,1)S(1)} %copy-done, bf16[64,32,128]{2,1,0:T(8,128)(2,1)S(1)} %copy-done.4, bf16[64,32,128]{2,1,0:T(8,128)(2,1)} %collective-permute-done.2.swap_ref, bf16[64,32,128]{2,1,0:T(8,128)(2,1)S(1)} %collective-permute-done.cross_ref, ...), custom_call_target="tpu_custom_call" | custom-call | flops 400000000 | bytes 6000000 | tf_op jit(solution)/shard_map/pallas_call | solution.py:432
Async XLA Ops:
  6.2 21.5 %collective-permute-start = (bf16[64,32,128]{2,1,0:T(8,128)(2,1)}, bf16[64,32,128]{2,1,0:T(8,128)(2,1)S(1)}, u32[]{:S(2)}, u32[]{:S(2)}) collective-permute-start(bf16[64,32,128]{2,1,0:T(8,128)(2,1)} %get-tuple-element.20), channel_id=1, source_target_pairs={{0,3},{3,0},{1,2},{2,1},{4,7},{7,4},{5,6},{6,5},{8,11},{11,8},{9,1... | collective-permute-start | bytes 1572872 | tf_op jit(solution)/shard_map/ppermute | solution.py:387
  17.6 10.1 %collective-permute-start.1 = (bf16[64,32,128]{2,1,0:T(8,128)(2,1)}, bf16[64,32,128]{2,1,0:T(8,128)(2,1)S(1)}, u32[]{:S(2)}, u32[]{:S(2)}) collective-permute-start(bf16[64,32,128]{2,1,0:T(8,128)(2,1)} %get-tuple-element.21.right_ref), channel_id=1, source_target_pairs={{0,1},{1,0},{7,6},{6,7},{8,9},{9,8},{15,14},{14,15},{16,17},{17,16... | collective-permute-start | bytes 1572872 | tf_op jit(solution)/shard_map/ppermute | solution.py:390
  18.3 13.6 %copy-start.3 = (bf16[64,32,128]{2,1,0:T(8,128)(2,1)S(1)}, bf16[64,32,128]{2,1,0:T(8,128)(2,1)}, u32[]{:S(2)}) copy-start(bf16[64,32,128]{2,1,0:T(8,128)(2,1)} %get-tuple-element.21.right_ref) | copy-start | bytes 1572868
  22.9 9.1 %copy-start.1 = (bf16[128,32,128]{2,1,0:T(8,128)(2,1)S(1)}, bf16[128,32,128]{2,1,0:T(8,128)(2,1)}, u32[]{:S(2)}) copy-start(bf16[128,32,128]{2,1,0:T(8,128)(2,1)} %get-tuple-element.25.left_ref) | copy-start | bytes 3145732
  22.9 16.2 %all-to-all-start = ((bf16[4,16,32,128]{3,2,1,0:T(8,128)(2,1)}), bf16[4,16,32,128]{3,2,1,0:T(8,128)(2,1)S(1)}, u32[]{:S(2)}, u32[]{:S(2)}) async-start(bf16[4,16,32,128]{3,2,1,0:T(8,128)(2,1)} %get-tuple-element.32), calls=%async_computation | async-start | bytes 1048576 | tf_op jit(solution)/shard_map/all_to_all | solution.py:405
  27.7 18.0 %collective-permute-start.3 = (bf16[64,32,128]{2,1,0:T(8,128)(2,1)S(1)}, bf16[64,32,128]{2,1,0:T(8,128)(2,1)}, u32[]{:S(2)}, u32[]{:S(2)}) collective-permute-start(bf16[64,32,128]{2,1,0:T(8,128)(2,1)S(1)} %collective-permute-done.cross_ref), channel_id=1, source_target_pairs={{3,2},{2,3},{4,5},{5,4},{11,10},{10,11},{12,13},{13,12},{19,18},{1... | collective-permute-start | bytes 1572872 | tf_op jit(solution)/shard_map/ppermute | solution.py:408
  30.5 15.3 %collective-permute-start.2 = (bf16[64,32,128]{2,1,0:T(8,128)(2,1)}, bf16[64,32,128]{2,1,0:T(8,128)(2,1)}, u32[]{:S(2)}, u32[]{:S(2)}) collective-permute-start(bf16[64,32,128]{2,1,0:T(8,128)(2,1)} %get-tuple-element.23.right_ref), channel_id=1, source_target_pairs={{0,1},{1,0},{7,6},{6,7},{8,9},{9,8},{15,14},{14,15},{16,17},{17,16... | collective-permute-start | bytes 1572872 | tf_op jit(solution)/shard_map/ppermute | solution.py:409
  31.9 7.2 %copy-start.11 = (bf16[256,512]{1,0:T(8,128)(2,1)S(1)}, bf16[256,512]{1,0:T(8,128)(2,1)}, u32[]{:S(2)}) copy-start(bf16[256,512]{1,0:T(8,128)(2,1)} %get-tuple-element.34.wcat_ref) | copy-start | bytes 786436
  33.6 0.8 %copy-start.5 = (f32[1024,128]{1,0:T(8,128)}, f32[1024,128]{1,0:T(8,128)S(1)}, u32[]{:S(2)}) copy-start(f32[1024,128]{1,0:T(8,128)S(1)} %get-tuple-element.27.sum_ref) | copy-start | bytes 1572868
  34.4 11.3 %collective-permute-start.4 = (bf16[64,16,128]{2,1,0:T(8,128)(2,1)}, bf16[64,16,128]{2,1,0:T(8,128)(2,1)S(1)}, u32[]{:S(2)}, u32[]{:S(2)}) collective-permute-start(bf16[64,16,128]{2,1,0:T(8,128)(2,1)} %get-tuple-element.28), channel_id=1, source_target_pairs={{0,3},{1,2},{7,4},{6,5},{8,11},{9,10},{15,12},{14,13},{16,19},{17,... | collective-permute-start | bytes 786440 | tf_op jit(solution)/shard_map/ppermute | solution.py:416
  39.1 0.7 %copy-start.12 = (f32[128]{0:T(128)S(1)}, f32[128]{0:T(128)}, u32[]{:S(2)}) copy-start(f32[128]{0:T(128)} %param.25) | copy-start | bytes 1540
  39.7 6.0 %copy-start = (bf16[32,128,128]{2,1,0:T(8,128)(2,1)S(1)}, bf16[32,128,128]{2,1,0:T(8,128)(2,1)}, u32[]{:S(2)}) copy-start(bf16[32,128,128]{2,1,0:T(8,128)(2,1)} %own_ref.1) | copy-start | bytes 3145732
  39.7 6.0 %copy-start.2 = (f32[16,128,128]{2,1,0:T(8,128)S(1)}, f32[16,128,128]{2,1,0:T(8,128)}, u32[]{:S(2)}) copy-start(f32[16,128,128]{2,1,0:T(8,128)} %get-tuple-element.31.gate_ref) | copy-start | bytes 3145732
  39.7 6.0 %copy-start.4 = (bf16[64,32,128]{2,1,0:T(8,128)(2,1)S(1)}, bf16[64,32,128]{2,1,0:T(8,128)(2,1)}, u32[]{:S(2)}) copy-start(bf16[64,32,128]{2,1,0:T(8,128)(2,1)} %get-tuple-element.23.right_ref) | copy-start | bytes 1572868
  39.7 6.0 %copy-start.6 = (f32[1024,128]{1,0:T(8,128)S(1)}, f32[1024,128]{1,0:T(8,128)}, u32[]{:S(2)}) copy-start(f32[1024,128]{1,0:T(8,128)} %copy-done.5) | copy-start | bytes 1572868
  39.8 6.0 %copy-start.7 = (bf16[128,128]{1,0:T(8,128)(2,1)S(1)}, bf16[128,128]{1,0:T(8,128)(2,1)}, u32[]{:S(2)}) copy-start(bf16[128,128]{1,0:T(8,128)(2,1)} %wt_ref.1) | copy-start | bytes 98308
  45.7 0.7 %copy-start.8 = (f32[128]{0:T(128)S(1)}, f32[128]{0:T(128)}, u32[]{:S(2)}) copy-start(f32[128]{0:T(128)} %param.30) | copy-start | bytes 1540
  45.7 0.7 %copy-start.9 = (f32[128]{0:T(128)S(1)}, f32[128]{0:T(128)}, u32[]{:S(2)}) copy-start(f32[128]{0:T(128)} %param.31) | copy-start | bytes 1540
  45.7 0.7 %copy-start.10 = (f32[128]{0:T(128)S(1)}, f32[128]{0:T(128)}, u32[]{:S(2)}) copy-start(f32[128]{0:T(128)} %param.33) | copy-start | bytes 1540

commit v4 on v3

--- a/solution.py
+++ b/solution.py
@@ -403,10 +403,10 @@
         couple_matrix, pair_gain, pair_bias, trimul_entry_matrices, offsets, pairwise_final_matrix,
     )
     arrived = lax.all_to_all(message, "dap", 0, 0, tiled=True)
-
-    crossed, swapped, upper = lax.optimization_barrier((crossed, swapped, upper))
+    upper, gate = lax.optimization_barrier((upper, gate))
+    swapped_upper = lax.ppermute(upper, both, swap)
+
     relayed = lax.ppermute(crossed, both, [(3, 2), (2, 3), (4, 5), (5, 4)])
-    swapped_upper = lax.ppermute(upper, both, swap)
     sums, given = call(
         partner_kernel,
         [SDS((1024, 128), F32), SDS((64, 16, 128), BF16)],

time: 51.2 us -> 49 us (0.957); the launches traced: 50.2 us -> 48.6 us
  waiting for transfers between devices: 6.59 us -> 4.92 us
    ppermute x1, waiting for transfers between devices: 3.16 us -> 1.52 us  [local(): taken = lax.ppermute(given, both, [(0, 3), (1, 2), (7, 4), (6, 5)])]
  transfers between devices with their start and end apart: 6 -> 6, of which waited for: 2 -> 2; matrix products, arithmetic and copies ran while one was open for 0% -> 0% of each run, Pallas kernels for 18% -> 19%
where the time goes in v4:
time: 49 us; the launch traced here: 48.6 us
  starting transfers between devices  22.4 us (46%)
  Pallas kernels  19 us (39%)
  waiting for transfers between devices  4.92 us (10%)
  local copies, waits for them, and re-layouts  2.11 us (4%)
    ppermute x1, starting transfers between devices, local(): lax.ppermute(cross, both, [(0, 3), (3, 0), (1, 2), (2, 1), (4, 7), (7, 4)...  11.4 us
    pallas_call x1, Pallas kernels, local(): call(sides_kernel, [block, half, half, half, SDS((8, 128), F32)], [SMEM,...  6.16 us
    all_to_all x1, starting transfers between devices, local(): arrived = lax.all_to_all(message, 'dap', 0, 0, tiled=True)  4.81 us
    pallas_call x1, Pallas kernels, local(): call(middle_kernel, [SDS((4, seqs, 32, 128), BF16), SDS((rows // 2, 128,...  4.58 us
    pallas_call x1, Pallas kernels, local(): call(triangle_kernel, SDS((rows, 64, 128), BF16), [VMEM] * 14, [pltpu.VME...  3.83 us
    all_to_all x1, waiting for transfers between devices, local(): arrived = lax.all_to_all(message, 'dap', 0, 0, tiled=True)  3.39 us
    pallas_call x1, Pallas kernels, local(): call(outer_kernel, SDS((rows // 2, 128, 128), BF16), [VMEM] * 3, [pltpu.V...  2.78 us
    ppermute x1, starting transfers between devices, local(): relayed = lax.ppermute(crossed, both, [(3, 2), (2, 3), (4, 5), (5, 4)])  2.75 us
  transfers between devices with their start and end apart: 6, of which 2 were waited for; matrix products, arithmetic and copies ran while one was open for 0% of the time, Pallas kernels for 19%

profile of v4, /device:TPU:6, one launch (start us, length us, event | category | flops | bytes accessed | tf_op | source)
XLA Modules:
  0.0 48.6 jit_solution(10092652059865874101)
XLA Ops:
  0.0 6.2 %shard_map.163 = (bf16[128,32,128]{2,1,0:T(8,128)(2,1)}, bf16[64,32,128]{2,1,0:T(8,128)(2,1)}, bf16[64,32,128]{2,1,0:T(8,128)(2,1)}, bf16[64,32,128]{2,1,0:T(8,128)(2,1)}, f32[8,128]{1,0:T(8,128)}) custom-call(s32[128]{0:T(128)} %present.1, bf16[32,128,128]{2,1,0:T(8,128)(2,1)} %own_ref.1, s32[1,128]{1,0:T(1,128)} %bitcast.17, f32[1,128]{1,0:T(1,128)} %bitcast.19, ...), custom_call_target="tpu_custom_call" | custom-call | flops 600000000 | bytes 4000000 | tf_op jit(solution)/shard_map/pallas_call | solution.py:373
  6.2 11.4 %collective-permute-start.1 = (bf16[64,32,128]{2,1,0:T(8,128)(2,1)}, bf16[64,32,128]{2,1,0:T(8,128)(2,1)S(1)}, u32[]{:S(2)}, u32[]{:S(2)}) collective-permute-start(bf16[64,32,128]{2,1,0:T(8,128)(2,1)} %get-tuple-element.20), channel_id=1, source_target_pairs={{0,3},{3,0},{1,2},{2,1},{4,7},{7,4},{5,6},{6,5},{8,11},{11,8},{9,1... | collective-permute-start | bytes 1572872 | tf_op jit(solution)/shard_map/ppermute | solution.py:387
  17.6 0.7 %collective-permute-start.3 = (bf16[64,32,128]{2,1,0:T(8,128)(2,1)}, bf16[64,32,128]{2,1,0:T(8,128)(2,1)S(1)}, u32[]{:S(2)}, u32[]{:S(2)}) collective-permute-start(bf16[64,32,128]{2,1,0:T(8,128)(2,1)} %get-tuple-element.26.right_ref), channel_id=1, source_target_pairs={{0,1},{1,0},{7,6},{6,7},{8,9},{9,8},{15,14},{14,15},{16,17},{17,16... | collective-permute-start | bytes 1572872 | tf_op jit(solution)/shard_map/ppermute | solution.py:390
  18.3 0.0 copy-start.3
  18.3 4.6 %shard_map.164 = (bf16[4,16,32,128]{3,2,1,0:T(8,128)(2,1)}, f32[16,128,128]{2,1,0:T(8,128)}, bf16[256,512]{1,0:T(8,128)(2,1)}) custom-call(bf16[16,128,256]{2,1,0:T(8,128)(2,1)} %homolog, s32[16,128]{1,0:T(8,128)} %flag.1, s32[1,128]{1,0:T(1,128)} %bitcast.18, f32[1,256]{1,0:T(1,128)} %bitcast.15, f32[1,256]{1,0:T(1,128)} %bitcast.16, ...), custom_call_target="tpu_custom_call" | custom-call | flops 300000000 | bytes 5000000 | tf_op jit(solution)/shard_map/pallas_call | solution.py:393
  22.9 0.0 copy-start.1
  22.9 4.8 %all-to-all-start = ((bf16[4,16,32,128]{3,2,1,0:T(8,128)(2,1)}), bf16[4,16,32,128]{3,2,1,0:T(8,128)(2,1)S(1)}, u32[]{:S(2)}, u32[]{:S(2)}) async-start(bf16[4,16,32,128]{3,2,1,0:T(8,128)(2,1)} %get-tuple-element.30), calls=%async_computation | async-start | bytes 1048576 | tf_op jit(solution)/shard_map/all_to_all | solution.py:405
  27.7 1.5 %collective-permute-start = (bf16[64,32,128]{2,1,0:T(8,128)(2,1)}, bf16[64,32,128]{2,1,0:T(8,128)(2,1)}, u32[]{:S(2)}, u32[]{:S(2)}) collective-permute-start(bf16[64,32,128]{2,1,0:T(8,128)(2,1)} %get-tuple-element.24.right_ref), channel_id=1, source_target_pairs={{0,1},{1,0},{7,6},{6,7},{8,9},{9,8},{15,14},{14,15},{16,17},{17,16... | collective-permute-start | bytes 1572872 | tf_op jit(solution)/shard_map/ppermute | solution.py:407
  29.1 0.0 collective-permute-done.1.cross_ref
  29.1 2.8 %collective-permute-start.2 = (bf16[64,32,128]{2,1,0:T(8,128)(2,1)S(1)}, bf16[64,32,128]{2,1,0:T(8,128)(2,1)}, u32[]{:S(2)}, u32[]{:S(2)}) collective-permute-start(bf16[64,32,128]{2,1,0:T(8,128)(2,1)S(1)} %collective-permute-done.1.cross_ref), channel_id=1, source_target_pairs={{3,2},{2,3},{4,5},{5,4},{11,10},{10,11},{12,13},{13,12},{19,18},{1... | collective-permute-start | bytes 1572872 | tf_op jit(solution)/shard_map/ppermute | solution.py:409
  31.9 0.0 collective-permute-done.3.swap_ref
  31.9 0.0 copy-done.3
  31.9 0.0 copy-done.1
  31.9 0.0 copy-start.11
  31.9 1.7 %shard_map.165 = (f32[1024,128]{1,0:T(8,128)S(1)}, bf16[64,16,128]{2,1,0:T(8,128)(2,1)}) custom-call(bf16[128,32,128]{2,1,0:T(8,128)(2,1)S(1)} %copy-done.1, bf16[64,32,128]{2,1,0:T(8,128)(2,1)S(1)} %collective-permute-done.1.cross_ref, bf16[64,32,128]{2,1,0:T(8,128)(2,1)S(1)} %copy-done.3, bf16[64,32,128]{2,1,0:T(8,128)(2,1)S(1)} %collective-permute-done.3.swap_ref), custom_call_target="tpu_custom_call" | custom-call | flops 200000000 | bytes 3000000 | tf_op jit(solution)/shard_map/pallas_call | solution.py:410
  33.6 0.0 copy-start.5
  33.6 0.8 %copy-done.5 = f32[1024,128]{1,0:T(8,128)} copy-done((f32[1024,128]{1,0:T(8,128)}, f32[1024,128]{1,0:T(8,128)S(1)}, u32[]{:S(2)}) %copy-start.5) | copy-done | bytes 524312
  34.4 1.3 %collective-permute-start.4 = (bf16[64,16,128]{2,1,0:T(8,128)(2,1)}, bf16[64,16,128]{2,1,0:T(8,128)(2,1)S(1)}, u32[]{:S(2)}, u32[]{:S(2)}) collective-permute-start(bf16[64,16,128]{2,1,0:T(8,128)(2,1)} %get-tuple-element.28), channel_id=1, source_target_pairs={{0,3},{1,2},{7,4},{6,5},{8,11},{9,10},{15,12},{14,13},{16,19},{17,... | collective-permute-start | bytes 786440 | tf_op jit(solution)/shard_map/ppermute | solution.py:416
  35.7 3.4 %all-to-all-done.m_ref = bf16[4,16,32,128]{3,2,1,0:T(8,128)(2,1)S(1)} async-done(((bf16[4,16,32,128]{3,2,1,0:T(8,128)(2,1)}), bf16[4,16,32,128]{3,2,1,0:T(8,128)(2,1)S(1)}, u32[]{:S(2)}, u32[]{:S(2)}) %all-to-all-start) | async-done | bytes 524320 | tf_op jit(solution)/shard_map/all_to_all | solution.py:405
  39.1 0.0 copy-start.12
  39.1 0.0 copy-done.11
  39.1 0.7 %copy-done.12 = f32[128]{0:T(128)S(1)} copy-done((f32[128]{0:T(128)S(1)}, f32[128]{0:T(128)}, u32[]{:S(2)}) %copy-start.12) | copy-done | bytes 536
  39.7 0.0 copy-start
  39.7 0.0 copy-start.2
  39.7 0.0 copy-start.4
  39.7 0.0 copy-start.6
  39.8 0.0 copy-start.7
  39.8 2.8 %shard_map.166.opm_ref = bf16[16,128,128]{2,1,0:T(8,128)(2,1)S(1)} custom-call(bf16[4,16,32,128]{3,2,1,0:T(8,128)(2,1)S(1)} %all-to-all-done.m_ref, bf16[256,512]{1,0:T(8,128)(2,1)S(1)} %copy-done.11, f32[1,128]{1,0:T(1,128)S(1)} %bitcast.13), custom_call_target="tpu_custom_call" | custom-call | flops 1600000000 | bytes 2000000 | tf_op jit(solution)/shard_map/pallas_call | solution.py:419
  42.6 0.0 collective-permute-done.swap_ref
  42.6 1.5 %collective-permute-done.4.taken_ref = bf16[64,16,128]{2,1,0:T(8,128)(2,1)S(1)} collective-permute-done((bf16[64,16,128]{2,1,0:T(8,128)(2,1)}, bf16[64,16,128]{2,1,0:T(8,128)(2,1)S(1)}, u32[]{:S(2)}, u32[]{:S(2)}) %collective-permute-start.4) | collective-permute-done | bytes 262176 | tf_op jit(solution)/shard_map/ppermute | solution.py:416
  44.1 0.0 collective-permute-done.2.relay_ref
  44.1 0.0 copy-start.8
  44.1 0.0 copy-start.9
  44.1 0.0 copy-start.10
  44.1 0.0 copy-done
  44.1 0.0 copy-done.2
  44.1 0.0 copy-done.4
  44.1 0.0 copy-done.6
  44.1 0.0 copy-done.7
  44.1 0.6 %copy-done.8 = f32[128]{0:T(128)S(1)} copy-done((f32[128]{0:T(128)S(1)}, f32[128]{0:T(128)}, u32[]{:S(2)}) %copy-start.8) | copy-done | bytes 536
  44.7 0.0 copy-done.9
  44.8 0.0 copy-done.10
  44.8 3.8 %shard_map.167 = bf16[32,64,128]{2,1,0:T(8,128)(2,1)} custom-call(bf16[32,128,128]{2,1,0:T(8,128)(2,1)S(1)} %copy-done, bf16[64,32,128]{2,1,0:T(8,128)(2,1)S(1)} %copy-done.4, bf16[64,32,128]{2,1,0:T(8,128)(2,1)} %collective-permute-done.swap_ref, bf16[64,32,128]{2,1,0:T(8,128)(2,1)S(1)} %collective-permute-done.1.cross_ref, ...), custom_call_target="tpu_custom_call" | custom-call | flops 400000000 | bytes 6000000 | tf_op jit(solution)/shard_map/pallas_call | solution.py:432
Async XLA Ops:
  6.2 23.0 %collective-permute-start.1 = (bf16[64,32,128]{2,1,0:T(8,128)(2,1)}, bf16[64,32,128]{2,1,0:T(8,128)(2,1)S(1)}, u32[]{:S(2)}, u32[]{:S(2)}) collective-permute-start(bf16[64,32,128]{2,1,0:T(8,128)(2,1)} %get-tuple-element.20), channel_id=1, source_target_pairs={{0,3},{3,0},{1,2},{2,1},{4,7},{7,4},{5,6},{6,5},{8,11},{11,8},{9,1... | collective-permute-start | bytes 1572872 | tf_op jit(solution)/shard_map/ppermute | solution.py:387
  17.6 14.3 %collective-permute-start.3 = (bf16[64,32,128]{2,1,0:T(8,128)(2,1)}, bf16[64,32,128]{2,1,0:T(8,128)(2,1)S(1)}, u32[]{:S(2)}, u32[]{:S(2)}) collective-permute-start(bf16[64,32,128]{2,1,0:T(8,128)(2,1)} %get-tuple-element.26.right_ref), channel_id=1, source_target_pairs={{0,1},{1,0},{7,6},{6,7},{8,9},{9,8},{15,14},{14,15},{16,17},{17,16... | collective-permute-start | bytes 1572872 | tf_op jit(solution)/shard_map/ppermute | solution.py:390
  18.3 13.6 %copy-start.3 = (bf16[64,32,128]{2,1,0:T(8,128)(2,1)S(1)}, bf16[64,32,128]{2,1,0:T(8,128)(2,1)}, u32[]{:S(2)}) copy-start(bf16[64,32,128]{2,1,0:T(8,128)(2,1)} %get-tuple-element.26.right_ref) | copy-start | bytes 1572868
  22.9 9.1 %copy-start.1 = (bf16[128,32,128]{2,1,0:T(8,128)(2,1)S(1)}, bf16[128,32,128]{2,1,0:T(8,128)(2,1)}, u32[]{:S(2)}) copy-start(bf16[128,32,128]{2,1,0:T(8,128)(2,1)} %get-tuple-element.25.left_ref) | copy-start | bytes 3145732
  22.9 16.2 %all-to-all-start = ((bf16[4,16,32,128]{3,2,1,0:T(8,128)(2,1)}), bf16[4,16,32,128]{3,2,1,0:T(8,128)(2,1)S(1)}, u32[]{:S(2)}, u32[]{:S(2)}) async-start(bf16[4,16,32,128]{3,2,1,0:T(8,128)(2,1)} %get-tuple-element.30), calls=%async_computation | async-start | bytes 1048576 | tf_op jit(solution)/shard_map/all_to_all | solution.py:405
  27.7 14.9 %collective-permute-start = (bf16[64,32,128]{2,1,0:T(8,128)(2,1)}, bf16[64,32,128]{2,1,0:T(8,128)(2,1)}, u32[]{:S(2)}, u32[]{:S(2)}) collective-permute-start(bf16[64,32,128]{2,1,0:T(8,128)(2,1)} %get-tuple-element.24.right_ref), channel_id=1, source_target_pairs={{0,1},{1,0},{7,6},{6,7},{8,9},{9,8},{15,14},{14,15},{16,17},{17,16... | collective-permute-start | bytes 1572872 | tf_op jit(solution)/shard_map/ppermute | solution.py:407
  29.1 14.9 %collective-permute-start.2 = (bf16[64,32,128]{2,1,0:T(8,128)(2,1)S(1)}, bf16[64,32,128]{2,1,0:T(8,128)(2,1)}, u32[]{:S(2)}, u32[]{:S(2)}) collective-permute-start(bf16[64,32,128]{2,1,0:T(8,128)(2,1)S(1)} %collective-permute-done.1.cross_ref), channel_id=1, source_target_pairs={{3,2},{2,3},{4,5},{5,4},{11,10},{10,11},{12,13},{13,12},{19,18},{1... | collective-permute-start | bytes 1572872 | tf_op jit(solution)/shard_map/ppermute | solution.py:409
  31.9 7.2 %copy-start.11 = (bf16[256,512]{1,0:T(8,128)(2,1)S(1)}, bf16[256,512]{1,0:T(8,128)(2,1)}, u32[]{:S(2)}) copy-start(bf16[256,512]{1,0:T(8,128)(2,1)} %get-tuple-element.32.wcat_ref) | copy-start | bytes 786436
  33.6 0.8 %copy-start.5 = (f32[1024,128]{1,0:T(8,128)}, f32[1024,128]{1,0:T(8,128)S(1)}, u32[]{:S(2)}) copy-start(f32[1024,128]{1,0:T(8,128)S(1)} %get-tuple-element.27.sum_ref) | copy-start | bytes 1572868
  34.4 9.7 %collective-permute-start.4 = (bf16[64,16,128]{2,1,0:T(8,128)(2,1)}, bf16[64,16,128]{2,1,0:T(8,128)(2,1)S(1)}, u32[]{:S(2)}, u32[]{:S(2)}) collective-permute-start(bf16[64,16,128]{2,1,0:T(8,128)(2,1)} %get-tuple-element.28), channel_id=1, source_target_pairs={{0,3},{1,2},{7,4},{6,5},{8,11},{9,10},{15,12},{14,13},{16,19},{17,... | collective-permute-start | bytes 786440 | tf_op jit(solution)/shard_map/ppermute | solution.py:416
  39.1 0.7 %copy-start.12 = (f32[128]{0:T(128)S(1)}, f32[128]{0:T(128)}, u32[]{:S(2)}) copy-start(f32[128]{0:T(128)} %param.25) | copy-start | bytes 1540
  39.7 4.4 %copy-start = (bf16[32,128,128]{2,1,0:T(8,128)(2,1)S(1)}, bf16[32,128,128]{2,1,0:T(8,128)(2,1)}, u32[]{:S(2)}) copy-start(bf16[32,128,128]{2,1,0:T(8,128)(2,1)} %own_ref.1) | copy-start | bytes 3145732
  39.7 4.4 %copy-start.2 = (f32[16,128,128]{2,1,0:T(8,128)S(1)}, f32[16,128,128]{2,1,0:T(8,128)}, u32[]{:S(2)}) copy-start(f32[16,128,128]{2,1,0:T(8,128)} %get-tuple-element.29.gate_ref) | copy-start | bytes 3145732
  39.7 4.4 %copy-start.4 = (bf16[64,32,128]{2,1,0:T(8,128)(2,1)S(1)}, bf16[64,32,128]{2,1,0:T(8,128)(2,1)}, u32[]{:S(2)}) copy-start(bf16[64,32,128]{2,1,0:T(8,128)(2,1)} %get-tuple-element.24.right_ref) | copy-start | bytes 1572868
  39.7 4.4 %copy-start.6 = (f32[1024,128]{1,0:T(8,128)S(1)}, f32[1024,128]{1,0:T(8,128)}, u32[]{:S(2)}) copy-start(f32[1024,128]{1,0:T(8,128)} %copy-done.5) | copy-start | bytes 1572868
  39.8 4.4 %copy-start.7 = (bf16[128,128]{1,0:T(8,128)(2,1)S(1)}, bf16[128,128]{1,0:T(8,128)(2,1)}, u32[]{:S(2)}) copy-start(bf16[128,128]{1,0:T(8,128)(2,1)} %wt_ref.1) | copy-start | bytes 98308
  44.1 0.7 %copy-start.8 = (f32[128]{0:T(128)S(1)}, f32[128]{0:T(128)}, u32[]{:S(2)}) copy-start(f32[128]{0:T(128)} %param.30) | copy-start | bytes 1540
  44.1 0.7 %copy-start.9 = (f32[128]{0:T(128)S(1)}, f32[128]{0:T(128)}, u32[]{:S(2)}) copy-start(f32[128]{0:T(128)} %param.31) | copy-start | bytes 1540
  44.1 0.7 %copy-start.10 = (f32[128]{0:T(128)S(1)}, f32[128]{0:T(128)}, u32[]{:S(2)}) copy-start(f32[128]{0:T(128)} %param.33) | copy-start | bytes 1540

commit v5 on v4

--- a/solution.py
+++ b/solution.py
@@ -143,7 +143,7 @@
 
 def sides_kernel(
     present, couple, window_ref, gain_ref, bias_ref, weight, offset,
-    left_ref, lower_ref, upper_ref, cross_ref, offset_out,
+    left_ref, right_ref, cross_ref, offset_out,
     couple_v, weight_v, offset_v, left_scr, right_scr, sems,
 ):
     rows = couple_v.shape[0]
@@ -179,7 +179,7 @@
         right = [right_scr[pl.ds(c + 64 * h, rows, stride=SIDE_PITCH), :].astype(BF16) for h in range(2)]
         for h in range(2):
             left_ref[c + 64 * h] = left[h]
-        lower_ref[c], upper_ref[c] = right
+            right_ref[c + 64 * h] = right[h]
         cross_ref[c] = jnp.where(member, right[1], left[0])
         return 0
 
@@ -293,8 +293,8 @@
         )
 
     def channel(c, _):
-        near = jnp.where(member, right_ref[c], relay_ref[c])
-        far = jnp.where(member, swap_ref[c], cross_ref[c])
+        near = jnp.where(member, right_ref[c + 64], relay_ref[c])
+        far = jnp.where(member, swap_ref[c + 64], cross_ref[c])
         lo, hi = jnp.where(even, near, far), jnp.where(even, far, near)
         prod = dot_nt(left_ref[c + 64], jnp.concatenate([lo, hi], axis=0))
         sums = jnp.concatenate([prod[0:16], prod[16:32]], axis=1)
@@ -370,9 +370,9 @@
     scratch = pltpu.VMEM((rows * SIDE_PITCH, 128), F32)
     half = SDS((64, rows, 128), BF16)
 
-    left, lower, upper, cross, offsets = call(
+    left, right, cross, offsets = call(
         sides_kernel,
-        [block, half, half, half, SDS((8, 128), F32)],
+        [block, block, half, SDS((8, 128), F32)],
         [SMEM, HBM, VMEM, VMEM, VMEM, HBM, HBM],
         [
             pltpu.VMEM(couple_matrix.shape, BF16), pltpu.VMEM((128, 640), BF16),
@@ -387,7 +387,7 @@
     crossed = lax.ppermute(
         cross, both, [(0, 3), (3, 0), (1, 2), (2, 1), (4, 7), (7, 4), (5, 6), (6, 5)]
     )
-    swapped = lax.ppermute(lower, both, swap)
+    swapped = lax.ppermute(right, both, swap)
 
     homolog, cross = lax.optimization_barrier((homolog_matrix, cross))
     message, gate, wcat = call(
@@ -403,8 +403,6 @@
         couple_matrix, pair_gain, pair_bias, trimul_entry_matrices, offsets, pairwise_final_matrix,
     )
     arrived = lax.all_to_all(message, "dap", 0, 0, tiled=True)
-    upper, gate = lax.optimization_barrier((upper, gate))
-    swapped_upper = lax.ppermute(upper, both, swap)
 
     relayed = lax.ppermute(crossed, both, [(3, 2), (2, 3), (4, 5), (5, 4)])
     sums, given = call(
@@ -412,7 +410,7 @@
         [SDS((1024, 128), F32), SDS((64, 16, 128), BF16)],
         [VMEM] * 4,
         flops=200_000_000, size=3_000_000,
-    )(left, crossed, lower, swapped)
+    )(left, crossed, right, swapped)
     taken = lax.ppermute(given, both, [(0, 3), (1, 2), (7, 4), (6, 5)])
 
     arrived, given = lax.optimization_barrier((arrived, given))
@@ -436,7 +434,7 @@
         [pltpu.VMEM((128 * SUM_PITCH, 128), F32)],
         flops=400_000_000, size=6_000_000,
     )(
-        couple_matrix, upper, swapped_upper, crossed, relayed, left, sums, taken, gate, opm,
+        couple_matrix, right, swapped, crossed, relayed, left, sums, taken, gate, opm,
         trimul_final_standardize_scaling[None], trimul_final_standardize_offset[None],
         trimul_final_matrix, trimul_final_offset[None],
     )

time: 49 us -> 51.7 us (1.055)
  Pallas kernels: 19 us -> 21.4 us
  waiting for transfers between devices: 4.92 us -> 2.87 us
  starting transfers between devices: 22.4 us -> 23.4 us
  local copies, waits for them, and re-layouts: 2.11 us -> 3.07 us
    all_to_all x1, waiting for transfers between devices: 3.39 us -> 0.63 us  [local(): arrived = lax.all_to_all(message, 'dap', 0, 0, tiled=True)]
    ppermute x2 -> x1, starting transfers between devices: 2.15 us -> 0.73 us  [local(): swapped = lax.ppermute(right, both, swap)]
    pallas_call x1, Pallas kernels: 2.78 us -> 4.04 us  [local(): call(outer_kernel, SDS((rows // 2, 128, 128), BF16), [VMEM] * 3, [pltpu.V...]
    ppermute x1, starting transfers between devices: 11.4 us -> 12.6 us  [local(): lax.ppermute(cross, both, [(0, 3), (3, 0), (1, 2), (2, 1), (4, 7), (7, 4)...]
    pallas_call x1, Pallas kernels: 1.67 us -> 2.73 us  [local(): call(partner_kernel, [SDS((1024, 128), F32), SDS((64, 16, 128), BF16)], [...]
    unnamed x26 -> x24, local copies, waits for them, and re-layouts: 2.11 us -> 3.07 us
    all_to_all x1, starting transfers between devices: 4.81 us -> 5.48 us  [local(): arrived = lax.all_to_all(message, 'dap', 0, 0, tiled=True)]
    ppermute x1, waiting for transfers between devices: 1.52 us -> 2.08 us  [local(): taken = lax.ppermute(given, both, [(0, 3), (1, 2), (7, 4), (6, 5)])]
  transfers between devices with their start and end apart: 6 -> 5, of which waited for: 2 -> 3; matrix products, arithmetic and copies ran while one was open for 0% -> 0% of each run, Pallas kernels for 19% -> 22%
where the time goes in v5:
time: 51.7 us; the launch traced here: 50.8 us
  starting transfers between devices  23.4 us (45%)
  Pallas kernels  21.4 us (41%)
  local copies, waits for them, and re-layouts  3.07 us (6%)
  waiting for transfers between devices  2.87 us (6%)
    ppermute x1, starting transfers between devices, local(): lax.ppermute(cross, both, [(0, 3), (3, 0), (1, 2), (2, 1), (4, 7), (7, 4)...  12.6 us
    pallas_call x1, Pallas kernels, local(): call(sides_kernel, [block, block, half, SDS((8, 128), F32)], [SMEM, HBM,...  6.17 us
    all_to_all x1, starting transfers between devices, local(): arrived = lax.all_to_all(message, 'dap', 0, 0, tiled=True)  5.48 us
    pallas_call x1, Pallas kernels, local(): call(middle_kernel, [SDS((4, seqs, 32, 128), BF16), SDS((rows // 2, 128,...  4.62 us
    pallas_call x1, Pallas kernels, local(): call(outer_kernel, SDS((rows // 2, 128, 128), BF16), [VMEM] * 3, [pltpu.V...  4.04 us
    pallas_call x1, Pallas kernels, local(): call(triangle_kernel, SDS((rows, 64, 128), BF16), [VMEM] * 14, [pltpu.VME...  3.83 us
    ppermute x1, starting transfers between devices, local(): relayed = lax.ppermute(crossed, both, [(3, 2), (2, 3), (4, 5), (5, 4)])  3.31 us
    unnamed x24, local copies, waits for them, and re-layouts  3.07 us
  transfers between devices with their start and end apart: 5, of which 3 were waited for; matrix products, arithmetic and copies ran while one was open for 0% of the time, Pallas kernels for 22%

profile of v5, /device:TPU:6, one launch (start us, length us, event | category | flops | bytes accessed | tf_op | source)
XLA Modules:
  0.0 50.8 jit_solution(12329493475440336984)
XLA Ops:
  0.0 6.2 %shard_map.163 = (bf16[128,32,128]{2,1,0:T(8,128)(2,1)}, bf16[128,32,128]{2,1,0:T(8,128)(2,1)}, bf16[64,32,128]{2,1,0:T(8,128)(2,1)}, f32[8,128]{1,0:T(8,128)}) custom-call(s32[128]{0:T(128)} %present.1, bf16[32,128,128]{2,1,0:T(8,128)(2,1)} %own_ref.1, s32[1,128]{1,0:T(1,128)} %bitcast.17, f32[1,128]{1,0:T(1,128)} %bitcast.19, f32[1,128]{1,0:T(1,128)} %bitcast.21, ...), custom_call_target="tpu_custom_call" | custom-call | flops 600000000 | bytes 4000000 | tf_op jit(solution)/shard_map/pallas_call | solution.py:373
  6.2 0.7 %collective-permute-start = (bf16[128,32,128]{2,1,0:T(8,128)(2,1)}, bf16[128,32,128]{2,1,0:T(8,128)(2,1)S(1)}, u32[]{:S(2)}, u32[]{:S(2)}) collective-permute-start(bf16[128,32,128]{2,1,0:T(8,128)(2,1)} %get-tuple-element.16.right_ref), channel_id=1, source_target_pairs={{0,1},{1,0},{7,6},{6,7},{8,9},{9,8},{15,14},{14,15},{16,17},{17,16... | collective-permute-start | bytes 3145736 | tf_op jit(solution)/shard_map/ppermute | solution.py:390
  6.9 12.6 %collective-permute-start.1 = (bf16[64,32,128]{2,1,0:T(8,128)(2,1)}, bf16[64,32,128]{2,1,0:T(8,128)(2,1)}, u32[]{:S(2)}, u32[]{:S(2)}) collective-permute-start(bf16[64,32,128]{2,1,0:T(8,128)(2,1)} %get-tuple-element.17), channel_id=1, source_target_pairs={{0,3},{3,0},{1,2},{2,1},{4,7},{7,4},{5,6},{6,5},{8,11},{11,8},{9,1... | collective-permute-start | bytes 1572872 | tf_op jit(solution)/shard_map/ppermute | solution.py:387
  19.5 0.0 copy-start.1
  19.5 4.6 %shard_map.165 = (bf16[4,16,32,128]{3,2,1,0:T(8,128)(2,1)}, f32[16,128,128]{2,1,0:T(8,128)}, bf16[256,512]{1,0:T(8,128)(2,1)}) custom-call(bf16[16,128,256]{2,1,0:T(8,128)(2,1)} %homolog, s32[16,128]{1,0:T(8,128)} %flag.1, s32[1,128]{1,0:T(1,128)} %bitcast.18, f32[1,256]{1,0:T(1,128)} %bitcast.15, f32[1,256]{1,0:T(1,128)} %bitcast.16, ...), custom_call_target="tpu_custom_call" | custom-call | flops 300000000 | bytes 5000000 | tf_op jit(solution)/shard_map/pallas_call | solution.py:393
  24.1 0.0 copy-start
  24.1 5.5 %all-to-all-start = ((bf16[4,16,32,128]{3,2,1,0:T(8,128)(2,1)}), bf16[4,16,32,128]{3,2,1,0:T(8,128)(2,1)}, u32[]{:S(2)}, u32[]{:S(2)}) async-start(bf16[4,16,32,128]{3,2,1,0:T(8,128)(2,1)} %get-tuple-element.24), calls=%async_computation | async-start | bytes 1048576 | tf_op jit(solution)/shard_map/all_to_all | solution.py:405
  29.6 0.2 collective-permute-done.1.cross_ref
  29.8 3.3 %collective-permute-start.2 = (bf16[64,32,128]{2,1,0:T(8,128)(2,1)}, bf16[64,32,128]{2,1,0:T(8,128)(2,1)}, u32[]{:S(2)}, u32[]{:S(2)}) collective-permute-start(bf16[64,32,128]{2,1,0:T(8,128)(2,1)} %collective-permute-done.1.cross_ref), channel_id=1, source_target_pairs={{3,2},{2,3},{4,5},{5,4},{11,10},{10,11},{12,13},{13,12},{19,18},{1... | collective-permute-start | bytes 1572872 | tf_op jit(solution)/shard_map/ppermute | solution.py:407
  33.1 0.0 collective-permute-done.swap_ref
  33.1 0.0 copy-done.1
  33.1 0.0 copy-done
  33.1 2.7 %shard_map.164 = (f32[1024,128]{1,0:T(8,128)S(1)}, bf16[64,16,128]{2,1,0:T(8,128)(2,1)}) custom-call(bf16[128,32,128]{2,1,0:T(8,128)(2,1)S(1)} %copy-done, bf16[64,32,128]{2,1,0:T(8,128)(2,1)} %collective-permute-done.1.cross_ref, bf16[128,32,128]{2,1,0:T(8,128)(2,1)S(1)} %copy-done.1, bf16[128,32,128]{2,1,0:T(8,128)(2,1)S(1)} %collective-permute-done.swap_ref), custom_call_target="tpu_custom_call" | custom-call | flops 200000000 | bytes 3000000 | tf_op jit(solution)/shard_map/pallas_call | solution.py:408
  35.9 0.0 copy-start.4
  35.9 0.8 %copy-done.4 = f32[1024,128]{1,0:T(8,128)} copy-done((f32[1024,128]{1,0:T(8,128)}, f32[1024,128]{1,0:T(8,128)S(1)}, u32[]{:S(2)}) %copy-start.4) | copy-done | bytes 524312
  36.7 1.3 %collective-permute-start.3 = (bf16[64,16,128]{2,1,0:T(8,128)(2,1)}, bf16[64,16,128]{2,1,0:T(8,128)(2,1)S(1)}, u32[]{:S(2)}, u32[]{:S(2)}) collective-permute-start(bf16[64,16,128]{2,1,0:T(8,128)(2,1)} %get-tuple-element.20), channel_id=1, source_target_pairs={{0,3},{1,2},{7,4},{6,5},{8,11},{9,10},{15,12},{14,13},{16,19},{17,... | collective-permute-start | bytes 786440 | tf_op jit(solution)/shard_map/ppermute | solution.py:414
  37.9 0.6 %all-to-all-done.m_ref = bf16[4,16,32,128]{3,2,1,0:T(8,128)(2,1)} async-done(((bf16[4,16,32,128]{3,2,1,0:T(8,128)(2,1)}), bf16[4,16,32,128]{3,2,1,0:T(8,128)(2,1)}, u32[]{:S(2)}, u32[]{:S(2)}) %all-to-all-start) | async-done | bytes 524320 | tf_op jit(solution)/shard_map/all_to_all | solution.py:405
  38.6 0.0 copy-start.11
  38.6 0.7 %copy-done.11 = f32[128]{0:T(128)S(1)} copy-done((f32[128]{0:T(128)S(1)}, f32[128]{0:T(128)}, u32[]{:S(2)}) %copy-start.11) | copy-done | bytes 536
  39.2 0.0 copy-start.10
  39.2 0.9 %copy-done.10 = bf16[256,512]{1,0:T(8,128)(2,1)S(1)} copy-done((bf16[256,512]{1,0:T(8,128)(2,1)S(1)}, bf16[256,512]{1,0:T(8,128)(2,1)}, u32[]{:S(2)}) %copy-start.10) | copy-done | bytes 262168
  40.2 0.0 copy-start.2
  40.2 0.0 copy-start.3
  40.2 0.0 copy-start.5
  40.2 0.0 copy-start.6
  40.2 4.0 %shard_map.166.opm_ref = bf16[16,128,128]{2,1,0:T(8,128)(2,1)S(1)} custom-call(bf16[4,16,32,128]{3,2,1,0:T(8,128)(2,1)} %all-to-all-done.m_ref, bf16[256,512]{1,0:T(8,128)(2,1)S(1)} %copy-done.10, f32[1,128]{1,0:T(1,128)S(1)} %bitcast.13), custom_call_target="tpu_custom_call" | custom-call | flops 1600000000 | bytes 2000000 | tf_op jit(solution)/shard_map/pallas_call | solution.py:417
  44.2 0.0 collective-permute-done.2.relay_ref
  44.3 2.1 %collective-permute-done.3.taken_ref = bf16[64,16,128]{2,1,0:T(8,128)(2,1)S(1)} collective-permute-done((bf16[64,16,128]{2,1,0:T(8,128)(2,1)}, bf16[64,16,128]{2,1,0:T(8,128)(2,1)S(1)}, u32[]{:S(2)}, u32[]{:S(2)}) %collective-permute-start.3) | collective-permute-done | bytes 262176 | tf_op jit(solution)/shard_map/ppermute | solution.py:414
  46.3 0.0 copy-start.7
  46.3 0.0 copy-start.8
  46.3 0.0 copy-start.9
  46.3 0.0 copy-done.2
  46.3 0.0 copy-done.3
  46.4 0.0 copy-done.5
  46.4 0.0 copy-done.6
  46.4 0.6 %copy-done.7 = f32[128]{0:T(128)S(1)} copy-done((f32[128]{0:T(128)S(1)}, f32[128]{0:T(128)}, u32[]{:S(2)}) %copy-start.7) | copy-done | bytes 536
  47.0 0.0 copy-done.8
  47.0 0.0 copy-done.9
  47.0 3.8 %shard_map.167 = bf16[32,64,128]{2,1,0:T(8,128)(2,1)} custom-call(bf16[32,128,128]{2,1,0:T(8,128)(2,1)S(1)} %copy-done.2, bf16[128,32,128]{2,1,0:T(8,128)(2,1)S(1)} %copy-done.1, bf16[128,32,128]{2,1,0:T(8,128)(2,1)S(1)} %collective-permute-done.swap_ref, bf16[64,32,128]{2,1,0:T(8,128)(2,1)} %collective-permute-done.1.cross_ref, ...), custom_call_target="tpu_custom_call" | custom-call | flops 400000000 | bytes 6000000 | tf_op jit(solution)/shard_map/pallas_call | solution.py:430
Async XLA Ops:
  6.2 26.9 %collective-permute-start = (bf16[128,32,128]{2,1,0:T(8,128)(2,1)}, bf16[128,32,128]{2,1,0:T(8,128)(2,1)S(1)}, u32[]{:S(2)}, u32[]{:S(2)}) collective-permute-start(bf16[128,32,128]{2,1,0:T(8,128)(2,1)} %get-tuple-element.16.right_ref), channel_id=1, source_target_pairs={{0,1},{1,0},{7,6},{6,7},{8,9},{9,8},{15,14},{14,15},{16,17},{17,16... | collective-permute-start | bytes 3145736 | tf_op jit(solution)/shard_map/ppermute | solution.py:390
  6.9 22.9 %collective-permute-start.1 = (bf16[64,32,128]{2,1,0:T(8,128)(2,1)}, bf16[64,32,128]{2,1,0:T(8,128)(2,1)}, u32[]{:S(2)}, u32[]{:S(2)}) collective-permute-start(bf16[64,32,128]{2,1,0:T(8,128)(2,1)} %get-tuple-element.17), channel_id=1, source_target_pairs={{0,3},{3,0},{1,2},{2,1},{4,7},{7,4},{5,6},{6,5},{8,11},{11,8},{9,1... | collective-permute-start | bytes 1572872 | tf_op jit(solution)/shard_map/ppermute | solution.py:387
  19.5 13.6 %copy-start.1 = (bf16[128,32,128]{2,1,0:T(8,128)(2,1)S(1)}, bf16[128,32,128]{2,1,0:T(8,128)(2,1)}, u32[]{:S(2)}) copy-start(bf16[128,32,128]{2,1,0:T(8,128)(2,1)} %get-tuple-element.16.right_ref) | copy-start | bytes 3145732
  24.1 9.0 %copy-start = (bf16[128,32,128]{2,1,0:T(8,128)(2,1)S(1)}, bf16[128,32,128]{2,1,0:T(8,128)(2,1)}, u32[]{:S(2)}) copy-start(bf16[128,32,128]{2,1,0:T(8,128)(2,1)} %get-tuple-element.18.left_ref) | copy-start | bytes 3145732
  24.1 14.4 %all-to-all-start = ((bf16[4,16,32,128]{3,2,1,0:T(8,128)(2,1)}), bf16[4,16,32,128]{3,2,1,0:T(8,128)(2,1)}, u32[]{:S(2)}, u32[]{:S(2)}) async-start(bf16[4,16,32,128]{3,2,1,0:T(8,128)(2,1)} %get-tuple-element.24), calls=%async_computation | async-start | bytes 1048576 | tf_op jit(solution)/shard_map/all_to_all | solution.py:405
  29.8 14.5 %collective-permute-start.2 = (bf16[64,32,128]{2,1,0:T(8,128)(2,1)}, bf16[64,32,128]{2,1,0:T(8,128)(2,1)}, u32[]{:S(2)}, u32[]{:S(2)}) collective-permute-start(bf16[64,32,128]{2,1,0:T(8,128)(2,1)} %collective-permute-done.1.cross_ref), channel_id=1, source_target_pairs={{3,2},{2,3},{4,5},{5,4},{11,10},{10,11},{12,13},{13,12},{19,18},{1... | collective-permute-start | bytes 1572872 | tf_op jit(solution)/shard_map/ppermute | solution.py:407
  35.9 0.8 %copy-start.4 = (f32[1024,128]{1,0:T(8,128)}, f32[1024,128]{1,0:T(8,128)S(1)}, u32[]{:S(2)}) copy-start(f32[1024,128]{1,0:T(8,128)S(1)} %get-tuple-element.19.sum_ref) | copy-start | bytes 1572868
  36.7 9.7 %collective-permute-start.3 = (bf16[64,16,128]{2,1,0:T(8,128)(2,1)}, bf16[64,16,128]{2,1,0:T(8,128)(2,1)S(1)}, u32[]{:S(2)}, u32[]{:S(2)}) collective-permute-start(bf16[64,16,128]{2,1,0:T(8,128)(2,1)} %get-tuple-element.20), channel_id=1, source_target_pairs={{0,3},{1,2},{7,4},{6,5},{8,11},{9,10},{15,12},{14,13},{16,19},{17,... | collective-permute-start | bytes 786440 | tf_op jit(solution)/shard_map/ppermute | solution.py:414
  38.6 0.7 %copy-start.11 = (f32[128]{0:T(128)S(1)}, f32[128]{0:T(128)}, u32[]{:S(2)}) copy-start(f32[128]{0:T(128)} %param.25) | copy-start | bytes 1540
  39.2 0.9 %copy-start.10 = (bf16[256,512]{1,0:T(8,128)(2,1)S(1)}, bf16[256,512]{1,0:T(8,128)(2,1)}, u32[]{:S(2)}) copy-start(bf16[256,512]{1,0:T(8,128)(2,1)} %get-tuple-element.26.wcat_ref) | copy-start | bytes 786436
  40.2 6.2 %copy-start.2 = (bf16[32,128,128]{2,1,0:T(8,128)(2,1)S(1)}, bf16[32,128,128]{2,1,0:T(8,128)(2,1)}, u32[]{:S(2)}) copy-start(bf16[32,128,128]{2,1,0:T(8,128)(2,1)} %own_ref.1) | copy-start | bytes 3145732
  40.2 6.2 %copy-start.3 = (f32[16,128,128]{2,1,0:T(8,128)S(1)}, f32[16,128,128]{2,1,0:T(8,128)}, u32[]{:S(2)}) copy-start(f32[16,128,128]{2,1,0:T(8,128)} %get-tuple-element.23.gate_ref) | copy-start | bytes 3145732
  40.2 6.2 %copy-start.5 = (f32[1024,128]{1,0:T(8,128)S(1)}, f32[1024,128]{1,0:T(8,128)}, u32[]{:S(2)}) copy-start(f32[1024,128]{1,0:T(8,128)} %copy-done.4) | copy-start | bytes 1572868
  40.2 6.2 %copy-start.6 = (bf16[128,128]{1,0:T(8,128)(2,1)S(1)}, bf16[128,128]{1,0:T(8,128)(2,1)}, u32[]{:S(2)}) copy-start(bf16[128,128]{1,0:T(8,128)(2,1)} %wt_ref.1) | copy-start | bytes 98308
  46.3 0.7 %copy-start.7 = (f32[128]{0:T(128)S(1)}, f32[128]{0:T(128)}, u32[]{:S(2)}) copy-start(f32[128]{0:T(128)} %param.30) | copy-start | bytes 1540
  46.3 0.7 %copy-start.8 = (f32[128]{0:T(128)S(1)}, f32[128]{0:T(128)}, u32[]{:S(2)}) copy-start(f32[128]{0:T(128)} %param.31) | copy-start | bytes 1540
  46.3 0.7 %copy-start.9 = (f32[128]{0:T(128)S(1)}, f32[128]{0:T(128)}, u32[]{:S(2)}) copy-start(f32[128]{0:T(128)} %param.33) | copy-start | bytes 1540
